TPU v7x, 32 devices: a whole 2x2x4 slice. The times are simulated.
32 devices in a mesh: space: 4 (over z), orb: 8 (over y, x, core).
Axes of the slice: x: 2, y: 2, z: 4, core: 2. Of those that a mesh axis runs over, the one named last changes fastest.
Arguments:
- orbitals: bfloat16 [128, 40, 1600], P(('space', 'orb')), may hold values from -6 to 6
- box_offset: int32 [128, 3], replicated, may hold values from 0 to 79, as said below
- send_index: int32 [32, 2, 8], P(('space', 'orb')), may hold values from 0 to 3
- pair_left: int32 [32, 2, 8], P(('space', 'orb')), may hold values from 0 to 3
Outputs:
- exchange_field: float32 [128, 40, 1600], P(('space', 'orb'))
Inputs may be any that keep to these rules, and one draw needn't show every extreme that they name: `box_offset`: box corners are cell coordinates on the periodic grid of 80 cells a side.
All inputs are finite; a program needn't handle non-finite values.
Results may differ from a plain program's by a relative error of at most 0.0008.
Values may be sent and summed in bfloat16 or wider, within the bound.
No kernel may reach another device: no remote copies, remote signals or barrier semaphores. Data moves between devices by JAX's collectives and lax.ppermute only.
A program may use at most 128 MiB of HBM per device.

v0:
```python
import functools

import jax
import jax.numpy as jnp
from jax import lax
from jax.experimental import pallas as pl
from jax.experimental.pallas import tpu as pltpu
from jax.sharding import PartitionSpec as P

B = 40
ITERS = 4
SCREEN = 0.25

GROUPS = 3
TILES = 14
LANES = 128
USED = GROUPS * B
SUB = 8
PLANES = B // SUB
CELLS = TILES * PLANES
CELL = 2 * SUB
HALF = B // 2
VMEM_BYTES = 52 * 2**20
FIELDS = 8


def lanes_of(shape):
    return lax.broadcasted_iota(jnp.int32, shape, len(shape) - 1)


def overlaps():
    pieces = []
    for b in range(B):
        group = b // TILES
        for flat in range(b * B // LANES, (b * B + B - 1) // LANES + 1):
            pieces.append((b, flat, b * B - flat * LANES - group * B))
    return pieces


def pack_body(box_ref, table_ref, first_ref, second_ref, stage):
    count = box_ref.shape[0]
    lane = lanes_of((B, LANES))
    for n in range(count):
        tiles = [jnp.zeros((B, LANES), jnp.float32) for _ in range(TILES)]
        loaded = {}
        for b, flat, shift in overlaps():
            if flat not in loaded:
                width = min(LANES, B * B - flat * LANES)
                part = box_ref[n, :, flat * LANES : flat * LANES + width].astype(jnp.float32)
                if width < LANES:
                    part = jnp.concatenate(
                        [part, jnp.zeros((B, LANES - width), jnp.float32)], axis=1
                    )
                stage[flat] = part
                loaded[flat] = jnp.concatenate(
                    [stage[flat, pl.ds(p, SUB, stride=PLANES), :] for p in range(PLANES)], axis=0
                )
            first = max(b * B, flat * LANES) - b * B + (b // TILES) * B
            last = min(b * B + B, flat * LANES + LANES) - b * B + (b // TILES) * B
            moved = pltpu.roll(loaded[flat], (-shift) % LANES, axis=1)
            keep = (lane >= first) & (lane < last)
            tiles[b % TILES] = jnp.where(keep, moved, tiles[b % TILES])
        if n == 0:
            tiles[0] = tiles[0] + table_ref[...]
        out_ref = first_ref if n < count // 2 else second_ref
        for t in range(TILES):
            out_ref[n % (count // 2), t] = tiles[t].astype(out_ref.dtype)


def pack(orbitals, table):
    count = orbitals.shape[0]
    return pl.pallas_call(
        pack_body,
        out_shape=[jax.ShapeDtypeStruct((count // 2, TILES, B, LANES), jnp.bfloat16)] * 2,
        in_specs=[pl.BlockSpec(memory_space=pltpu.VMEM)] * 2,
        out_specs=[pl.BlockSpec(memory_space=pltpu.VMEM)] * 2,
        scratch_shapes=[pltpu.VMEM((-(-B * B // LANES), B, LANES), jnp.float32)],
        compiler_params=pltpu.CompilerParams(vmem_limit_bytes=VMEM_BYTES),
        name="pack",
    )(orbitals, table)


def finish_body(count, slots, field_ref, near_ref, far_ref, row_ref, out_ref, total, stage):
    lane = lanes_of((B, LANES))
    for n in range(count):
        for t in range(TILES):
            total[n, t] = field_ref[n, t] + far_ref[n, t].astype(jnp.float32)

    def add(j, carry):
        row = row_ref[j]
        for t in range(TILES):
            total[row, t] += near_ref[j, t].astype(jnp.float32)
        return carry

    lax.fori_loop(0, slots, add, 0)
    for n in range(count):
        flats = {}
        for b, flat, shift in overlaps():
            first = max(b * B, flat * LANES) - flat * LANES
            last = min(b * B + B, flat * LANES + LANES) - flat * LANES
            moved = pltpu.roll(total[n, b % TILES], shift % LANES, axis=1)
            keep = (lane >= first) & (lane < last)
            before = flats.get(flat)
            flats[flat] = moved if before is None else jnp.where(keep, moved, before)
        for flat, value in flats.items():
            for p in range(PLANES):
                stage[flat, pl.ds(p, SUB, stride=PLANES), :] = value[p * SUB : p * SUB + SUB]
            width = min(LANES, B * B - flat * LANES)
            out_ref[n, :, flat * LANES : flat * LANES + width] = stage[flat, :, :width]


def finish(field, near, far, rows):
    count, slots = field.shape[0], near.shape[0]
    vmem = pl.BlockSpec(memory_space=pltpu.VMEM)
    return pl.pallas_call(
        functools.partial(finish_body, count, slots),
        out_shape=jax.ShapeDtypeStruct((count, B, B * B), jnp.float32),
        in_specs=[vmem, vmem, vmem, pl.BlockSpec(memory_space=pltpu.SMEM)],
        out_specs=vmem,
        scratch_shapes=[
            pltpu.VMEM((count, TILES, B, LANES), jnp.float32),
            pltpu.VMEM((-(-B * B // LANES), B, LANES), jnp.float32),
        ],
        compiler_params=pltpu.CompilerParams(vmem_limit_bytes=VMEM_BYTES),
        name="finish",
    )(field, near, far, rows)


def geometry(offset_ref, left, right, grid_cells):
    shift, live = [], jnp.int32(1)
    for axis in range(3):
        gap = offset_ref[3 * right + axis] - offset_ref[3 * left + axis] + grid_cells // 2
        gap = jnp.where(gap < 0, gap + grid_cells, gap)
        gap = jnp.where(gap >= grid_cells, gap - grid_cells, gap) - grid_cells // 2
        live = jnp.where((gap > HALF) | (gap < -HALF), 0, live)
        shift.append(gap)
    return shift, live


def lane_group(lane):
    return sum(jnp.where(lane >= B * (i + 1), 1, 0) for i in range(GROUPS))


def wrapped(shift, size):
    from_zero = B * size - shift
    quotient = (from_zero * (2**16 // size + 1)) >> 16
    start, turn = from_zero - size * quotient, quotient - B
    pairs = []
    for i in range(size):
        over = jnp.where(start + i >= size, 1, 0)
        pairs.append((start + i - size * over, turn + over))
    return pairs


def put_padded(pad, t, p, value):
    start = (t * PLANES + p) * CELL + SUB
    pad[start : start + SUB, :] = value


def displaced(pad, shift):
    lane = lanes_of((SUB, LANES))
    group = lane_group(lane)
    source_col = lane - group * B - shift[2]
    col_ok = (source_col >= 0) & (source_col < B) & (lane < USED)
    source_row = jnp.where(col_ok, TILES * group - shift[1], -2 * B)
    rows = [p * CELL + SUB + turn for p, turn in wrapped(shift[0], PLANES)]
    for t, (source, turn) in enumerate(wrapped(shift[1], TILES)):
        keep = (source_row + t >= 0) & (source_row + t < B)
        if t >= B - TILES * (GROUPS - 1):
            keep = keep & (lane < USED - B)
        amount = (shift[2] - B * turn + 2 * LANES) & (LANES - 1)
        tile = []
        for p in range(PLANES):
            block = pad[pl.ds(source * (PLANES * CELL) + rows[p], SUB), :]
            tile.append(jnp.where(keep, pltpu.roll(block, amount, axis=1), 0.0))
        yield t, tile


def tree_sum(values):
    while len(values) > 1:
        paired = [a + b for a, b in zip(values[::2], values[1::2])]
        values = paired + ([values[-1]] if len(values) % 2 else [])
    return values[0]


def blocks(value):
    return [value[p * SUB : p * SUB + SUB] for p in range(PLANES)]


def cell(t, p):
    start = (t * PLANES + p) * SUB
    return slice(start, start + SUB)


def make_operator():
    lane = lanes_of((SUB, LANES))
    sublane = lax.broadcasted_iota(jnp.int32, (SUB, LANES), 0)
    column = lane - B * lane_group(lane)
    has_before = (column > 0) & (lane < USED)
    has_after = (column < B - 1) & (lane < USED)
    not_first = lane >= B
    not_last = lane < USED - B
    has_above = sublane > 0
    has_below = sublane < SUB - 1

    def operator(t, before, here, after):
        if t == 0:
            before = [jnp.where(not_first, pltpu.roll(v, B, axis=1), 0.0) for v in before]
        if t == TILES - 1:
            after = [jnp.where(not_last, pltpu.roll(v, LANES - B, axis=1), 0.0) for v in after]
        result = []
        for p in range(PLANES):
            if p == 0:
                above = jnp.where(has_above, pltpu.roll(here[PLANES - 1], 1, axis=0), 0.0)
            else:
                above = here[p - 1]
            if p == PLANES - 1:
                below = jnp.where(has_below, pltpu.roll(here[0], SUB - 1, axis=0), 0.0)
            else:
                below = here[p + 1]
            prior = jnp.where(has_before, pltpu.roll(here[p], 1, axis=1), 0.0)
            following = jnp.where(has_after, pltpu.roll(here[p], LANES - 1, axis=1), 0.0)
            around = (above + below) + (before[p] + after[p]) + (prior + following)
            value = (6.0 + SCREEN) * here[p] - around
            if t == B - TILES * (GROUPS - 1):
                value = jnp.where(not_last, value, 0.0)
            result.append(value)
        return result

    return operator


def side_by_side(first, last, body):
    def pair(i, carry):
        for _ in zip(body(first + 2 * i, 0), body(first + 2 * i + 1, 1)):
            pass
        return carry

    lax.fori_loop(0, (last - first) >> 1, pair, 0)

    @pl.when(((last - first) & 1) == 1)
    def _():
        for _ in body(last - 1, 0):
            pass


def put_sum(sums, kind, m, value):
    sums[kind, pl.ds(m, 1), :] = jnp.sum(value, axis=0, keepdims=True)


def solve(used, directions, residuals, images, sums, steps, ratios):
    operator = make_operator()

    for k in range(ITERS):
        last = k == ITERS - 1
        source = directions[0] if k == 1 else residuals[k % 2]
        target = residuals[(k + 1) % 2]

        def stencil(m, side, k=k, last=last, source=source, target=target):
            squares = []
            if k > 0:
                step = jnp.broadcast_to(steps[k - 1, pl.ds(m, 1), :], (SUB, LANES))
                ratio = jnp.broadcast_to(ratios[pl.ds(m, 1), :], (SUB, LANES))

            def stored(t):
                return [directions[k][m, cell(t, p), :] for p in range(PLANES)]

            def fetch(t):
                if k == 0:
                    return stored(t)
                values, parts = [], []
                for p in range(PLANES):
                    left = source[m, cell(t, p), :] - step * images[(k - 1) % 2][m, cell(t, p), :]
                    if not last:
                        target[m, cell(t, p), :] = left
                    parts.append(left * left)
                    value = left + ratio * directions[k - 1][m, cell(t, p), :]
                    directions[k][m, cell(t, p), :] = value
                    values.append(value)
                squares.append(tree_sum(parts))
                if len(squares) == 2:
                    squares[:] = [squares[0] + squares[1]]
                return values

            before, here = fetch(TILES - 1), fetch(0)
            total = spread = None
            for t in range(TILES):
                after = fetch(t + 1) if t < TILES - 2 else stored((t + 1) % TILES)
                applied = operator(t, before, here, after)
                if not last:
                    for p in range(PLANES):
                        images[k % 2][m, cell(t, p), :] = applied[p]
                    part = tree_sum([x * x for x in applied])
                    spread = part if spread is None else spread + part
                part = tree_sum([x * y for x, y in zip(here, applied)])
                total = part if total is None else total + part
                before, here = here, after
                yield
            put_sum(sums, 1, m, total)
            if not last:
                put_sum(sums, 2, m, spread)
            if k > 0:
                put_sum(sums, 0, m, squares[0])
            yield

        side_by_side(0, used, stencil)
        norm, product, square = (
            jnp.broadcast_to(jnp.sum(sums[kind], axis=1, keepdims=True), sums.shape[1:])
            for kind in range(3)
        )
        step = norm / product
        steps[k] = step
        if not last:
            ratios[...] = jnp.maximum(step * step * square - norm, 0.0) / norm


def run_slots(used, nears, fars, shift_of, left_of, right_of, near_to, far_to, held, scratch):
    pads, shifted, sums, steps, ratios, *boxes = scratch
    residuals, images, directions = boxes[:2], boxes[2:4], boxes[4:]

    def box(row, t):
        return blocks(held[row, t].astype(jnp.float32))

    def load(m, side):
        pad = pads.at[side]
        left, right = left_of(m), right_of(m)
        for t in range(TILES):
            for p, block in enumerate(box(right, t)):
                put_padded(pad, t, p, block)
            yield
        total = None
        for t, moved in displaced(pad, shift_of(m)):
            squares = []
            for p, value in enumerate(box(left, t)):
                shifted[m, cell(t, p), :] = moved[p]
                density = moved[p] * value
                directions[0][m, cell(t, p), :] = density
                squares.append(density * density)
            part = tree_sum(squares)
            total = part if total is None else total + part
            yield
        put_sum(sums, 0, m, total)
        yield

    side_by_side(0, used, load)
    solve(used, directions, residuals, images, sums, steps, ratios)

    def unload(near, far):
        def one(m, side):
            pad = pads.at[side]
            left = left_of(m)
            weights = [
                jnp.broadcast_to(steps[k, pl.ds(m, 1), :], (SUB, LANES)) for k in range(ITERS)
            ]
            put_near = near_to(m) if near else None
            put_far = far_to(m) if far else None
            for t in range(TILES):
                solved = [
                    tree_sum([w * d[m, cell(t, p), :] for w, d in zip(weights, directions)])
                    for p in range(PLANES)
                ]
                if near:
                    terms = [v * shifted[m, cell(t, p), :] for p, v in enumerate(solved)]
                    put_near(t, jnp.concatenate(terms, axis=0))
                if far:
                    for p, value in enumerate(box(left, t)):
                        put_padded(pad, t, p, solved[p] * value)
                yield
            if far:
                for t, moved in displaced(pad, [-s for s in shift_of(m)]):
                    put_far(t, jnp.concatenate(moved, axis=0))
                    yield

        return one

    if nears is fars:
        side_by_side(*nears, unload(True, True))
    else:
        side_by_side(*nears, unload(True, False))
        side_by_side(*fars, unload(False, True))


def slot_scratch(batch):
    row = pltpu.VMEM((batch, LANES), jnp.float32)
    box = pltpu.VMEM((batch, CELLS * SUB, LANES), jnp.float32)
    return [
        pltpu.SMEM((batch * FIELDS,), jnp.int32),
        pltpu.VMEM((2, CELLS * CELL + SUB, LANES), jnp.float32),
        box,
        pltpu.VMEM((3, batch, LANES), jnp.float32),
        pltpu.VMEM((ITERS, batch, LANES), jnp.float32),
        row,
    ] + [box] * (4 + ITERS)


def clear(ref):
    for n in range(ref.shape[0]):
        for t in range(TILES):
            ref[n, t] = jnp.zeros((B, LANES), ref.dtype)


def append(listed, used, values):
    for i, value in enumerate(values):
        listed[used * FIELDS + i] = value


def adding(ref, row):
    def put(t, value):
        ref[row, t] += value

    return put


def piece_copies(pieces, index, held, slot, sem):
    part = pieces[0].shape[0]
    for h, piece in enumerate(pieces):

        @pl.when((index >= h * part) & (index < (h + 1) * part))
        def _(h=h, piece=piece):
            pltpu.make_async_copy(piece.at[index - h * part], held.at[slot], sem).start()


def wait_box(pieces, held, slot, sem):
    pltpu.make_async_copy(pieces[0].at[0], held.at[slot], sem).wait()


def read_tables(meta, orbs, me, count, index_ref):
    free = LANES - USED
    lines = orbs // free
    bits = count.bit_length() - 1
    row = lax.broadcasted_iota(jnp.int32, (B, LANES), 0)
    lane = lanes_of((B, LANES)) - USED

    def digits(value, length):
        value = value.astype(jnp.int32)
        for _ in range(length):
            rest = value >> bits if count == 1 << bits else lax.div(value, count)
            yield value - rest * count
            value = rest

    weight = jnp.zeros((B, LANES), jnp.float32)
    for place, kind in enumerate((0, 2, 3)):
        chosen = (row - kind * lines) * free + lane == me
        chosen = chosen & (lane >= 0)
        weight = jnp.where(chosen, float(count**place), weight)
    for k in range(orbs):
        source = jnp.bitwise_xor(me, k)
        total = jnp.sum(meta[k].astype(jnp.float32) * weight)
        for kind, value in enumerate(digits(total, 3)):
            index_ref[kind * orbs + source] = value
    weight = jnp.zeros((B, LANES), jnp.float32)
    for place in range(free):
        weight = jnp.where(lane == place, float(count**place), weight)
    arrived = meta[orbs].astype(jnp.float32) * weight
    for line in range(lines):
        total = jnp.sum(jnp.where(row == lines + line, arrived, 0.0))
        for place, value in enumerate(digits(total, free)):
            index_ref[3 * orbs + line * free + place] = value


def forward_body(orbs, count, grid_cells, where_ref, offset_ref, *refs):
    pieces = [refs[2 * k : 2 * k + 2] for k in range(orbs)]
    incoming = refs[2 * orbs : 2 * orbs + 2]
    near_ref, far_ref, index_ref, meta, held, far_sum, meta_sem, box_sem, listed = refs[
        2 * orbs + 2 : 2 * orbs + 11
    ]
    scratch = refs[2 * orbs + 11 :]
    batch = listed.shape[0] // FIELDS
    part = count // 2
    me = where_ref[2]
    first_left, first_right = where_ref[0], where_ref[1]

    tables = [
        pltpu.make_async_copy(source[0].at[0, 0], meta.at[k], meta_sem.at[k])
        for k, source in enumerate(pieces + [incoming])
    ]
    for copy in tables:
        copy.start()
    rights = [
        pltpu.make_async_copy(
            incoming[n // part].at[n % part], held.at[orbs + n], box_sem.at[orbs + n]
        )
        for n in range(count)
    ]
    for copy in rights:
        copy.start()
    scratch[0][...] = jnp.zeros(scratch[0].shape, jnp.float32)
    clear(far_sum)
    for copy in tables:
        copy.wait()
    read_tables(meta, orbs, me, count, index_ref)
    for k in range(orbs):
        source = jnp.bitwise_xor(me, k)
        piece_copies(pieces[k], index_ref[2 * orbs + source], held, source, box_sem.at[k])

    def run(i, carry):
        def gather(j, used):
            slot = i * batch + j
            left, right = slot * count + index_ref[2 * orbs + slot], index_ref[3 * orbs + slot]
            shift, live = geometry(
                offset_ref, first_left + left, first_right + right, grid_cells
            )

            @pl.when(live == 1)
            def _():
                append(listed, used, [slot, orbs + right, *shift])

            @pl.when(live == 0)
            def _():
                for t in range(TILES):
                    near_ref[slot, t] = jnp.zeros((B, LANES), near_ref.dtype)

            return used + live

        used = lax.fori_loop(0, batch, gather, jnp.int32(0))

        @pl.when(i == 0)
        def _():
            for k in range(orbs):
                wait_box(pieces[k], held, jnp.bitwise_xor(me, k), box_sem.at[k])
            for copy in rights:
                copy.wait()

        def shift_of(m):
            return [listed[m * FIELDS + 2 + axis] for axis in range(3)]

        def near_to(m):
            row = listed[m * FIELDS]

            def put(t, value):
                near_ref[row, t] = value.astype(near_ref.dtype)

            return put

        def far_to(m):
            return adding(far_sum, listed[m * FIELDS + 1] - orbs)

        every = (0, used)
        run_slots(
            used, every, every, shift_of,
            lambda m: listed[m * FIELDS], lambda m: listed[m * FIELDS + 1],
            near_to, far_to, held, scratch,
        )
        return carry

    lax.fori_loop(0, orbs // batch, run, 0)
    for n in range(count):
        for t in range(TILES):
            far_ref[n, t] = far_sum[n, t].astype(far_ref.dtype)


def forward_pairs(where, offsets, pieces, incoming, count, grid_cells):
    orbs = len(pieces)
    vmem, smem, left = (pl.BlockSpec(memory_space=m) for m in (pltpu.VMEM, pltpu.SMEM, pl.ANY))
    shape = (TILES, B, LANES)
    return pl.pallas_call(
        functools.partial(forward_body, orbs, count, grid_cells),
        out_shape=(
            jax.ShapeDtypeStruct((orbs,) + shape, jnp.bfloat16),
            jax.ShapeDtypeStruct((count,) + shape, jnp.bfloat16),
            jax.ShapeDtypeStruct((4 * orbs,), jnp.int32),
        ),
        in_specs=[smem] * 2 + [left] * (2 * orbs + 2),
        out_specs=(vmem, vmem, smem),
        scratch_shapes=[
            pltpu.VMEM((orbs + 1, B, LANES), jnp.bfloat16),
            pltpu.VMEM((orbs + count,) + shape, jnp.bfloat16),
            pltpu.VMEM((count,) + shape, jnp.float32),
            pltpu.SemaphoreType.DMA((orbs + 1,)),
            pltpu.SemaphoreType.DMA((orbs + count,)),
        ] + slot_scratch(8),
        compiler_params=pltpu.CompilerParams(vmem_limit_bytes=VMEM_BYTES),
        name="forward_pairs",
    )(where, offsets, *[half for piece in pieces for half in piece], *incoming)


def group_body(orbs, count, grid_cells, where_ref, offset_ref, mine_ref, sent_ref, index_ref, *refs):
    pieces = [refs[2 * k : 2 * k + 2] for k in range(orbs)]
    field, held, sem, listed = refs[2 * orbs : 2 * orbs + 4]
    scratch = refs[2 * orbs + 4 :]
    half = listed.shape[0] // FIELDS // 2
    part = count // 2
    first, me = where_ref[0], where_ref[2]
    mine = me * count
    own = 2 * orbs

    for k in range(orbs):
        source = jnp.bitwise_xor(me, k)
        piece_copies(pieces[k], index_ref[source], held, source, sem.at[k])
        piece_copies(pieces[k], index_ref[orbs + source], held, orbs + source, sem.at[orbs + k])
    owned = [
        pltpu.make_async_copy(pieces[0][n // part].at[n % part], held.at[own + n], sem.at[own + n])
        for n in range(count)
    ]
    for copy in owned:
        copy.start()
    scratch[0][...] = jnp.zeros(scratch[0].shape, jnp.float32)
    clear(field)

    def run(i, carry):
        def listing(near):
            def gather(j, used):
                slot = i * half + ((me + 1 + j) & (half - 1))
                if near:
                    left, right = mine + mine_ref[slot], slot * count + index_ref[slot]
                    boxes = [own + mine_ref[slot], slot]
                else:
                    left, right = slot * count + index_ref[orbs + slot], mine + sent_ref[slot]
                    boxes = [orbs + slot, own + sent_ref[slot]]
                shift, live = geometry(offset_ref, first + left, first + right, grid_cells)
                if not near:
                    live = jnp.where(slot == me, 0, live)
                else:
                    boxes[1] = jnp.where(slot == me, own + index_ref[slot], boxes[1])

                @pl.when(live == 1)
                def _():
                    append(listed, used, boxes + [*shift])

                return used + live

            return gather

        near_count = lax.fori_loop(0, half, listing(True), jnp.int32(0))
        used = lax.fori_loop(0, half, listing(False), near_count)
        left, right = mine + mine_ref[me], mine + index_ref[me]
        inside = geometry(offset_ref, first + left, first + right, grid_cells)[1]
        inside = jnp.where((me >= i * half) & (me < (i + 1) * half), inside, 0)

        @pl.when(i == 0)
        def _():
            for k in range(orbs):
                source = jnp.bitwise_xor(me, k)
                wait_box(pieces[k], held, source, sem.at[k])
                wait_box(pieces[k], held, orbs + source, sem.at[orbs + k])
            for copy in owned:
                copy.wait()

        def shift_of(m):
            return [listed[m * FIELDS + 2 + axis] for axis in range(3)]

        def near_to(m):
            return adding(field, listed[m * FIELDS] - own)

        def far_to(m):
            return adding(field, listed[m * FIELDS + 1] - own)

        run_slots(
            used, (0, near_count), (near_count - inside, used), shift_of,
            lambda m: listed[m * FIELDS], lambda m: listed[m * FIELDS + 1],
            near_to, far_to, held, scratch,
        )
        return carry

    lax.fori_loop(0, orbs // half, run, 0)


def group_pairs(where, offsets, mine, sent, index, pieces, count, grid_cells):
    orbs = len(pieces)
    vmem, smem, left = (pl.BlockSpec(memory_space=m) for m in (pltpu.VMEM, pltpu.SMEM, pl.ANY))
    shape = (TILES, B, LANES)
    return pl.pallas_call(
        functools.partial(group_body, orbs, count, grid_cells),
        out_shape=jax.ShapeDtypeStruct((count,) + shape, jnp.float32),
        in_specs=[smem] * 5 + [left] * (2 * orbs),
        out_specs=vmem,
        scratch_shapes=[
            pltpu.VMEM((2 * orbs + count,) + shape, jnp.bfloat16),
            pltpu.SemaphoreType.DMA((2 * orbs + count,)),
        ] + slot_scratch(16),
        compiler_params=pltpu.CompilerParams(vmem_limit_bytes=VMEM_BYTES),
        name="group_pairs",
    )(where, offsets, mine, sent, index, *[half for piece in pieces for half in piece])


def along_space(block, distance):
    size = lax.axis_size("space")
    return lax.ppermute(block, "space", [((i - distance) % size, i) for i in range(size)])


def group_exchange(packed, orbs):
    bits = [1 << i for i in range(orbs.bit_length() - 1)]
    orders = (bits[1:] + bits[:1], bits[:0:-1] + bits[:1])
    halves = []
    for block, order in zip(packed, orders):
        known = {0: block}
        for bit in order:
            route = [(i, i ^ bit) for i in range(orbs)]
            for k in list(known):
                known[k ^ bit] = lax.ppermute(known[k], "orb", route)
        halves.append(known)
    return [[known[k] for known in halves] for k in range(orbs)]


def per_device(orbitals, box_offset, send_index, pair_left):
    count = orbitals.shape[0]
    spaces, orbs = lax.axis_size("space"), lax.axis_size("orb")
    grid_cells = spaces * HALF
    space, orb = lax.axis_index("space"), lax.axis_index("orb")
    group_first = space * orbs * count
    offsets = box_offset.reshape(-1)

    free = LANES - USED
    entries = jnp.concatenate([send_index[0].reshape(-1), pair_left[0].reshape(-1)])
    lines = 4 * orbs // free
    table = jnp.pad(
        entries.astype(jnp.float32).reshape(lines, free), ((0, B - lines), (USED, 0))
    )
    packed = pack(orbitals, table)

    incoming = [along_space(half, -1) for half in packed]
    pieces = group_exchange(packed, orbs)
    where = jnp.stack([group_first, ((space + 1) % spaces * orbs + orb) * count, orb])
    near, far, index = forward_pairs(where, offsets, pieces, incoming, count, grid_cells)
    near = lax.all_to_all(near, "orb", split_axis=0, concat_axis=0, tiled=True)
    far = along_space(far, 1)
    field = group_pairs(
        where, offsets, pair_left[0, 0], send_index[0, 0], index, pieces, count, grid_cells
    )
    return finish(field, near, far, pair_left[0, 1])


def solution(mesh):
    split = P(("space", "orb"), None, None)
    return jax.shard_map(
        per_device, mesh=mesh, in_specs=(split, P(), split, split), out_specs=split,
        check_vma=False,
    )
```

profile of v0, /device:TPU:25, one launch (start us, length us, event | category | flops | bytes accessed | tf_op | source)
XLA Modules:
  0.0 73.2 jit_solution(11349310058180044695)
XLA Ops:
  0.0 0.7 add_convert_fusion
  0.8 1.0 %copy-done.1 = bf16[4,40,1600]{2,1,0:T(8,128)(2,1)S(1)} copy-done((bf16[4,40,1600]{2,1,0:T(8,128)(2,1)S(1)}, bf16[4,40,1600]{2,1,0:T(8,128)(2,1)}, u32[]{:S(2)}) %copy-start.1) | copy-done | bytes 512024
  1.8 0.6 pack.1
  2.6 1.2 %collective-permute-start.6 = (bf16[2,14,40,128]{3,2,1,0:T(8,128)(2,1)S(1)}, bf16[2,14,40,128]{3,2,1,0:T(8,128)(2,1)S(1)}, u32[]{:S(2)}, u32[]{:S(2)}) collective-permute-start(bf16[2,14,40,128]{3,2,1,0:T(8,128)(2,1)S(1)} %get-tuple-element.10.refs_0_), channel_id=1, source_target_pairs={{0,4},{1,5},{2,6},{3,7},{4,0},{5,1},{6,2},{7,3},{8,12},{9,13},{10,... | collective-permute-start | bytes 860168 | tf_op jit(solution)/shard_map/ppermute | solution.py:690
  3.9 1.2 %collective-permute-start.2 = (bf16[2,14,40,128]{3,2,1,0:T(8,128)(2,1)S(1)}, bf16[2,14,40,128]{3,2,1,0:T(8,128)(2,1)S(1)}, u32[]{:S(2)}, u32[]{:S(2)}) collective-permute-start(bf16[2,14,40,128]{3,2,1,0:T(8,128)(2,1)S(1)} %get-tuple-element.10.refs_0_), channel_id=1, source_target_pairs={{0,2},{1,3},{2,0},{3,1},{4,6},{5,7},{6,4},{7,5},{8,10},{9,11},{10,... | collective-permute-start | bytes 860168 | tf_op jit(solution)/shard_map/ppermute | solution.py:690
  5.1 1.5 %collective-permute-start = (bf16[2,14,40,128]{3,2,1,0:T(8,128)(2,1)S(1)}, bf16[2,14,40,128]{3,2,1,0:T(8,128)(2,1)S(1)}, u32[]{:S(2)}, u32[]{:S(2)}) collective-permute-start(bf16[2,14,40,128]{3,2,1,0:T(8,128)(2,1)S(1)} %get-tuple-element.10.refs_0_), channel_id=1, source_target_pairs={{0,1},{1,0},{2,3},{3,2},{4,5},{5,4},{6,7},{7,6},{8,9},{9,8},{10,11... | collective-permute-start | bytes 860168 | tf_op jit(solution)/shard_map/ppermute | solution.py:690
  6.8 5.2 %collective-permute-done.14.refs_16_ = bf16[2,14,40,128]{3,2,1,0:T(8,128)(2,1)S(1)} collective-permute-done((bf16[2,14,40,128]{3,2,1,0:T(8,128)(2,1)S(1)}, bf16[2,14,40,128]{3,2,1,0:T(8,128)(2,1)S(1)}, u32[]{:S(2)}, u32[]{:S(2)}) %collective-permute-start.14) | collective-permute-done | bytes 286752 | tf_op jit(solution)/shard_map/ppermute | solution.py:678
  12.0 1.2 %collective-permute-start.7 = (bf16[2,14,40,128]{3,2,1,0:T(8,128)(2,1)S(1)}, bf16[2,14,40,128]{3,2,1,0:T(8,128)(2,1)S(1)}, u32[]{:S(2)}, u32[]{:S(2)}) collective-permute-start(bf16[2,14,40,128]{3,2,1,0:T(8,128)(2,1)S(1)} %get-tuple-element.11.refs_1_), channel_id=1, source_target_pairs={{0,4},{1,5},{2,6},{3,7},{4,0},{5,1},{6,2},{7,3},{8,12},{9,13},{10,... | collective-permute-start | bytes 860168 | tf_op jit(solution)/shard_map/ppermute | solution.py:690
  13.2 1.3 %collective-permute-start.3 = (bf16[2,14,40,128]{3,2,1,0:T(8,128)(2,1)S(1)}, bf16[2,14,40,128]{3,2,1,0:T(8,128)(2,1)S(1)}, u32[]{:S(2)}, u32[]{:S(2)}) collective-permute-start(bf16[2,14,40,128]{3,2,1,0:T(8,128)(2,1)S(1)} %get-tuple-element.11.refs_1_), channel_id=1, source_target_pairs={{0,2},{1,3},{2,0},{3,1},{4,6},{5,7},{6,4},{7,5},{8,10},{9,11},{10,... | collective-permute-start | bytes 860168 | tf_op jit(solution)/shard_map/ppermute | solution.py:690
  14.5 3.3 %collective-permute-start.1 = (bf16[2,14,40,128]{3,2,1,0:T(8,128)(2,1)S(1)}, bf16[2,14,40,128]{3,2,1,0:T(8,128)(2,1)S(1)}, u32[]{:S(2)}, u32[]{:S(2)}) collective-permute-start(bf16[2,14,40,128]{3,2,1,0:T(8,128)(2,1)S(1)} %get-tuple-element.11.refs_1_), channel_id=1, source_target_pairs={{0,1},{1,0},{2,3},{3,2},{4,5},{5,4},{6,7},{7,6},{8,9},{9,8},{10,11... | collective-permute-start | bytes 860168 | tf_op jit(solution)/shard_map/ppermute | solution.py:690
  18.1 1.2 %collective-permute-start.10 = (bf16[2,14,40,128]{3,2,1,0:T(8,128)(2,1)S(1)}, bf16[2,14,40,128]{3,2,1,0:T(8,128)(2,1)S(1)}, u32[]{:S(2)}, u32[]{:S(2)}) collective-permute-start(bf16[2,14,40,128]{3,2,1,0:T(8,128)(2,1)S(1)} %collective-permute-done.2.refs_4_), channel_id=1, source_target_pairs={{0,4},{1,5},{2,6},{3,7},{4,0},{5,1},{6,2},{7,3},{8,12},{9,13},{10,... | collective-permute-start | bytes 860168 | tf_op jit(solution)/shard_map/ppermute | solution.py:690
  19.4 1.2 %collective-permute-start.11 = (bf16[2,14,40,128]{3,2,1,0:T(8,128)(2,1)S(1)}, bf16[2,14,40,128]{3,2,1,0:T(8,128)(2,1)S(1)}, u32[]{:S(2)}, u32[]{:S(2)}) collective-permute-start(bf16[2,14,40,128]{3,2,1,0:T(8,128)(2,1)S(1)} %collective-permute-done.7.refs_9_), channel_id=1, source_target_pairs={{0,2},{1,3},{2,0},{3,1},{4,6},{5,7},{6,4},{7,5},{8,10},{9,11},{10,... | collective-permute-start | bytes 860168 | tf_op jit(solution)/shard_map/ppermute | solution.py:690
  20.6 2.7 %collective-permute-start.4 = (bf16[2,14,40,128]{3,2,1,0:T(8,128)(2,1)S(1)}, bf16[2,14,40,128]{3,2,1,0:T(8,128)(2,1)S(1)}, u32[]{:S(2)}, u32[]{:S(2)}) collective-permute-start(bf16[2,14,40,128]{3,2,1,0:T(8,128)(2,1)S(1)} %collective-permute-done.2.refs_4_), channel_id=1, source_target_pairs={{0,1},{1,0},{2,3},{3,2},{4,5},{5,4},{6,7},{7,6},{8,9},{9,8},{10,11... | collective-permute-start | bytes 860168 | tf_op jit(solution)/shard_map/ppermute | solution.py:690
  23.3 0.5 collective-permute-start.5
  23.8 1.3 %collective-permute-done.10.refs_12_ = bf16[2,14,40,128]{3,2,1,0:T(8,128)(2,1)S(1)} collective-permute-done((bf16[2,14,40,128]{3,2,1,0:T(8,128)(2,1)S(1)}, bf16[2,14,40,128]{3,2,1,0:T(8,128)(2,1)S(1)}, u32[]{:S(2)}, u32[]{:S(2)}) %collective-permute-start.10) | collective-permute-done | bytes 286752 | tf_op jit(solution)/shard_map/ppermute | solution.py:690
  25.0 2.4 %collective-permute-start.12 = (bf16[2,14,40,128]{3,2,1,0:T(8,128)(2,1)S(1)}, bf16[2,14,40,128]{3,2,1,0:T(8,128)(2,1)}, u32[]{:S(2)}, u32[]{:S(2)}) collective-permute-start(bf16[2,14,40,128]{3,2,1,0:T(8,128)(2,1)S(1)} %collective-permute-done.10.refs_12_), channel_id=1, source_target_pairs={{0,1},{1,0},{2,3},{3,2},{4,5},{5,4},{6,7},{7,6},{8,9},{9,8},{10,11... | collective-permute-start | bytes 860168 | tf_op jit(solution)/shard_map/ppermute | solution.py:690
  27.4 1.6 %collective-permute-start.13 = (bf16[2,14,40,128]{3,2,1,0:T(8,128)(2,1)S(1)}, bf16[2,14,40,128]{3,2,1,0:T(8,128)(2,1)}, u32[]{:S(2)}, u32[]{:S(2)}) collective-permute-start(bf16[2,14,40,128]{3,2,1,0:T(8,128)(2,1)S(1)} %collective-permute-done.11.refs_13_), channel_id=1, source_target_pairs={{0,1},{1,0},{2,3},{3,2},{4,5},{5,4},{6,7},{7,6},{8,9},{9,8},{10,11... | collective-permute-start | bytes 860168 | tf_op jit(solution)/shard_map/ppermute | solution.py:690
  29.0 0.8 %copy.5 = s32[128,3]{1,0:T(8,128)S(1)} copy(s32[128,3]{0,1:T(4,128)} %param.5) | data formatting | bytes 3072 | tf_op args[1]
  30.4 9.5 %forward_pairs.1 = (bf16[8,14,40,128]{3,2,1,0:T(8,128)(2,1)}, bf16[4,14,40,128]{3,2,1,0:T(8,128)(2,1)}, s32[32]{0:T(128)S(1)}) custom-call(s32[3]{0:T(128)S(1)} %pad_add_fusion.where_ref, s32[384]{0:T(512)S(1)} %reshape.8.offset_ref, bf16[2,14,40,128]{3,2,1,0:T(8,128)(2,1)S(1)} %get-tuple-element.10.refs_0_, ...), custom_call_target="tpu_custom_call" | custom-call | tf_op jit(solution)/shard_map/forward_pairs/pallas_call | solution.py:556
  40.0 4.5 %all-to-all-start = ((bf16[8,14,40,128]{3,2,1,0:T(8,128)(2,1)}), bf16[8,14,40,128]{3,2,1,0:T(8,128)(2,1)}, u32[]{:S(2)}, u32[]{:S(2)}) async-start(bf16[8,14,40,128]{3,2,1,0:T(8,128)(2,1)} %get-tuple-element.13), calls=%async_computation | async-start | bytes 2293760 | tf_op jit(solution)/shard_map/all_to_all | solution.py:715
  44.5 4.2 %collective-permute-start.16 = (bf16[4,14,40,128]{3,2,1,0:T(8,128)(2,1)S(1)}, bf16[4,14,40,128]{3,2,1,0:T(8,128)(2,1)S(1)}, u32[]{:S(2)}, u32[]{:S(2)}) collective-permute-start(bf16[4,14,40,128]{3,2,1,0:T(8,128)(2,1)S(1)} %copy-done.11), channel_id=1, source_target_pairs={{24,0},{0,8},{8,16},{16,24},{25,1},{1,9},{9,17},{17,25},{26,2},{2,... | collective-permute-start | bytes 1720328 | tf_op jit(solution)/shard_map/ppermute | solution.py:678
  48.7 19.7 %group_pairs.1.field_ref = f32[4,14,40,128]{3,2,1,0:T(8,128)} custom-call(s32[3]{0:T(128)S(1)} %pad_add_fusion.where_ref, s32[384]{0:T(512)S(1)} %reshape.8.offset_ref, s32[8]{0:T(128)S(1)} %get-tuple-element.16.mine_ref, s32[8]{0:T(128)S(1)} %get-tuple-element.17.sent_ref, s32[32]{0:T(128)S(1)} %get-tuple-element.12.index_ref, ...), custom_call_target="tpu_custom_call" | custom-call | tf_op jit(solution)/shard_map/group_pairs/pallas_call | solution.py:662
  68.5 1.2 %copy-done = f32[4,14,40,128]{3,2,1,0:T(8,128)S(1)} copy-done((f32[4,14,40,128]{3,2,1,0:T(8,128)S(1)}, f32[4,14,40,128]{3,2,1,0:T(8,128)}, u32[]{:S(2)}) %copy-start) | copy-done | bytes 1146904
  69.7 3.5 %finish.1 = f32[4,40,1600]{2,1,0:T(8,128)} custom-call(f32[4,14,40,128]{3,2,1,0:T(8,128)S(1)} %copy-done, bf16[8,14,40,128]{3,2,1,0:T(8,128)(2,1)} %all-to-all-done.near_ref, bf16[4,14,40,128]{3,2,1,0:T(8,128)(2,1)S(1)} %collective-permute-done.16.far_ref, s32[8]{0:T(128)S(1)} %get-tuple-element.15.row_ref), custom_call_target="tpu_custom_call" | custom-call | tf_op jit(solution)/shard_map/finish/pallas_call | solution.py:115
  (46 shorter events, 1.4 us)
Async XLA Ops:
  2.4 9.6 %collective-permute-start.14 = (bf16[2,14,40,128]{3,2,1,0:T(8,128)(2,1)S(1)}, bf16[2,14,40,128]{3,2,1,0:T(8,128)(2,1)S(1)}, u32[]{:S(2)}, u32[]{:S(2)}) collective-permute-start(bf16[2,14,40,128]{3,2,1,0:T(8,128)(2,1)S(1)} %get-tuple-element.10.refs_0_), channel_id=1, source_target_pairs={{8,0},{16,8},{24,16},{0,24},{9,1},{17,9},{25,17},{1,25},{10,2},{18... | collective-permute-start | bytes 860168 | tf_op jit(solution)/shard_map/ppermute | solution.py:678
  2.6 10.6 %collective-permute-start.6 = (bf16[2,14,40,128]{3,2,1,0:T(8,128)(2,1)S(1)}, bf16[2,14,40,128]{3,2,1,0:T(8,128)(2,1)S(1)}, u32[]{:S(2)}, u32[]{:S(2)}) collective-permute-start(bf16[2,14,40,128]{3,2,1,0:T(8,128)(2,1)S(1)} %get-tuple-element.10.refs_0_), channel_id=1, source_target_pairs={{0,4},{1,5},{2,6},{3,7},{4,0},{5,1},{6,2},{7,3},{8,12},{9,13},{10,... | collective-permute-start | bytes 860168 | tf_op jit(solution)/shard_map/ppermute | solution.py:690
  3.9 10.6 %collective-permute-start.2 = (bf16[2,14,40,128]{3,2,1,0:T(8,128)(2,1)S(1)}, bf16[2,14,40,128]{3,2,1,0:T(8,128)(2,1)S(1)}, u32[]{:S(2)}, u32[]{:S(2)}) collective-permute-start(bf16[2,14,40,128]{3,2,1,0:T(8,128)(2,1)S(1)} %get-tuple-element.10.refs_0_), channel_id=1, source_target_pairs={{0,2},{1,3},{2,0},{3,1},{4,6},{5,7},{6,4},{7,5},{8,10},{9,11},{10,... | collective-permute-start | bytes 860168 | tf_op jit(solution)/shard_map/ppermute | solution.py:690
  5.1 12.7 %collective-permute-start = (bf16[2,14,40,128]{3,2,1,0:T(8,128)(2,1)S(1)}, bf16[2,14,40,128]{3,2,1,0:T(8,128)(2,1)S(1)}, u32[]{:S(2)}, u32[]{:S(2)}) collective-permute-start(bf16[2,14,40,128]{3,2,1,0:T(8,128)(2,1)S(1)} %get-tuple-element.10.refs_0_), channel_id=1, source_target_pairs={{0,1},{1,0},{2,3},{3,2},{4,5},{5,4},{6,7},{7,6},{8,9},{9,8},{10,11... | collective-permute-start | bytes 860168 | tf_op jit(solution)/shard_map/ppermute | solution.py:690
  6.6 11.5 %collective-permute-start.15 = (bf16[2,14,40,128]{3,2,1,0:T(8,128)(2,1)S(1)}, bf16[2,14,40,128]{3,2,1,0:T(8,128)(2,1)S(1)}, u32[]{:S(2)}, u32[]{:S(2)}) collective-permute-start(bf16[2,14,40,128]{3,2,1,0:T(8,128)(2,1)S(1)} %get-tuple-element.11.refs_1_), channel_id=1, source_target_pairs={{8,0},{16,8},{24,16},{0,24},{9,1},{17,9},{25,17},{1,25},{10,2},{18... | collective-permute-start | bytes 860168 | tf_op jit(solution)/shard_map/ppermute | solution.py:678
  12.0 7.4 %collective-permute-start.7 = (bf16[2,14,40,128]{3,2,1,0:T(8,128)(2,1)S(1)}, bf16[2,14,40,128]{3,2,1,0:T(8,128)(2,1)S(1)}, u32[]{:S(2)}, u32[]{:S(2)}) collective-permute-start(bf16[2,14,40,128]{3,2,1,0:T(8,128)(2,1)S(1)} %get-tuple-element.11.refs_1_), channel_id=1, source_target_pairs={{0,4},{1,5},{2,6},{3,7},{4,0},{5,1},{6,2},{7,3},{8,12},{9,13},{10,... | collective-permute-start | bytes 860168 | tf_op jit(solution)/shard_map/ppermute | solution.py:690
  13.2 17.2 %copy-start.2 = (bf16[2,14,40,128]{3,2,1,0:T(8,128)(2,1)}, bf16[2,14,40,128]{3,2,1,0:T(8,128)(2,1)S(1)}, u32[]{:S(2)}) copy-start(bf16[2,14,40,128]{3,2,1,0:T(8,128)(2,1)S(1)} %collective-permute-done.6.refs_8_) | copy-start | bytes 860164
  13.2 7.4 %collective-permute-start.3 = (bf16[2,14,40,128]{3,2,1,0:T(8,128)(2,1)S(1)}, bf16[2,14,40,128]{3,2,1,0:T(8,128)(2,1)S(1)}, u32[]{:S(2)}, u32[]{:S(2)}) collective-permute-start(bf16[2,14,40,128]{3,2,1,0:T(8,128)(2,1)S(1)} %get-tuple-element.11.refs_1_), channel_id=1, source_target_pairs={{0,2},{1,3},{2,0},{3,1},{4,6},{5,7},{6,4},{7,5},{8,10},{9,11},{10,... | collective-permute-start | bytes 860168 | tf_op jit(solution)/shard_map/ppermute | solution.py:690
  14.5 8.8 %collective-permute-start.1 = (bf16[2,14,40,128]{3,2,1,0:T(8,128)(2,1)S(1)}, bf16[2,14,40,128]{3,2,1,0:T(8,128)(2,1)S(1)}, u32[]{:S(2)}, u32[]{:S(2)}) collective-permute-start(bf16[2,14,40,128]{3,2,1,0:T(8,128)(2,1)S(1)} %get-tuple-element.11.refs_1_), channel_id=1, source_target_pairs={{0,1},{1,0},{2,3},{3,2},{4,5},{5,4},{6,7},{7,6},{8,9},{9,8},{10,11... | collective-permute-start | bytes 860168 | tf_op jit(solution)/shard_map/ppermute | solution.py:690
  17.7 5.5 %collective-permute-start.8 = (bf16[2,14,40,128]{3,2,1,0:T(8,128)(2,1)S(1)}, bf16[2,14,40,128]{3,2,1,0:T(8,128)(2,1)S(1)}, u32[]{:S(2)}, u32[]{:S(2)}) collective-permute-start(bf16[2,14,40,128]{3,2,1,0:T(8,128)(2,1)S(1)} %collective-permute-done.6.refs_8_), channel_id=1, source_target_pairs={{0,1},{1,0},{2,3},{3,2},{4,5},{5,4},{6,7},{7,6},{8,9},{9,8},{10,11... | collective-permute-start | bytes 860168 | tf_op jit(solution)/shard_map/ppermute | solution.py:690
  18.1 6.9 %collective-permute-start.10 = (bf16[2,14,40,128]{3,2,1,0:T(8,128)(2,1)S(1)}, bf16[2,14,40,128]{3,2,1,0:T(8,128)(2,1)S(1)}, u32[]{:S(2)}, u32[]{:S(2)}) collective-permute-start(bf16[2,14,40,128]{3,2,1,0:T(8,128)(2,1)S(1)} %collective-permute-done.2.refs_4_), channel_id=1, source_target_pairs={{0,4},{1,5},{2,6},{3,7},{4,0},{5,1},{6,2},{7,3},{8,12},{9,13},{10,... | collective-permute-start | bytes 860168 | tf_op jit(solution)/shard_map/ppermute | solution.py:690
  19.3 11.0 %copy-start.3 = (bf16[2,14,40,128]{3,2,1,0:T(8,128)(2,1)}, bf16[2,14,40,128]{3,2,1,0:T(8,128)(2,1)S(1)}, u32[]{:S(2)}) copy-start(bf16[2,14,40,128]{3,2,1,0:T(8,128)(2,1)S(1)} %collective-permute-done.7.refs_9_) | copy-start | bytes 860164
  19.4 8.1 %collective-permute-start.11 = (bf16[2,14,40,128]{3,2,1,0:T(8,128)(2,1)S(1)}, bf16[2,14,40,128]{3,2,1,0:T(8,128)(2,1)S(1)}, u32[]{:S(2)}, u32[]{:S(2)}) collective-permute-start(bf16[2,14,40,128]{3,2,1,0:T(8,128)(2,1)S(1)} %collective-permute-done.7.refs_9_), channel_id=1, source_target_pairs={{0,2},{1,3},{2,0},{3,1},{4,6},{5,7},{6,4},{7,5},{8,10},{9,11},{10,... | collective-permute-start | bytes 860168 | tf_op jit(solution)/shard_map/ppermute | solution.py:690
  20.6 9.5 %collective-permute-start.4 = (bf16[2,14,40,128]{3,2,1,0:T(8,128)(2,1)S(1)}, bf16[2,14,40,128]{3,2,1,0:T(8,128)(2,1)S(1)}, u32[]{:S(2)}, u32[]{:S(2)}) collective-permute-start(bf16[2,14,40,128]{3,2,1,0:T(8,128)(2,1)S(1)} %collective-permute-done.2.refs_4_), channel_id=1, source_target_pairs={{0,1},{1,0},{2,3},{3,2},{4,5},{5,4},{6,7},{7,6},{8,9},{9,8},{10,11... | collective-permute-start | bytes 860168 | tf_op jit(solution)/shard_map/ppermute | solution.py:690
  23.2 6.9 %collective-permute-start.9 = (bf16[2,14,40,128]{3,2,1,0:T(8,128)(2,1)S(1)}, bf16[2,14,40,128]{3,2,1,0:T(8,128)(2,1)}, u32[]{:S(2)}, u32[]{:S(2)}) collective-permute-start(bf16[2,14,40,128]{3,2,1,0:T(8,128)(2,1)S(1)} %collective-permute-done.7.refs_9_), channel_id=1, source_target_pairs={{0,1},{1,0},{2,3},{3,2},{4,5},{5,4},{6,7},{7,6},{8,9},{9,8},{10,11... | collective-permute-start | bytes 860168 | tf_op jit(solution)/shard_map/ppermute | solution.py:690
  23.2 7.1 %copy-start.4 = (bf16[2,14,40,128]{3,2,1,0:T(8,128)(2,1)}, bf16[2,14,40,128]{3,2,1,0:T(8,128)(2,1)S(1)}, u32[]{:S(2)}) copy-start(bf16[2,14,40,128]{3,2,1,0:T(8,128)(2,1)S(1)} %collective-permute-done.8.refs_10_) | copy-start | bytes 860164
  23.3 6.9 %collective-permute-start.5 = (bf16[2,14,40,128]{3,2,1,0:T(8,128)(2,1)S(1)}, bf16[2,14,40,128]{3,2,1,0:T(8,128)(2,1)}, u32[]{:S(2)}, u32[]{:S(2)}) collective-permute-start(bf16[2,14,40,128]{3,2,1,0:T(8,128)(2,1)S(1)} %collective-permute-done.3.refs_5_), channel_id=1, source_target_pairs={{0,1},{1,0},{2,3},{3,2},{4,5},{5,4},{6,7},{7,6},{8,9},{9,8},{10,11... | collective-permute-start | bytes 860168 | tf_op jit(solution)/shard_map/ppermute | solution.py:690
  25.0 5.3 %copy-start.5 = (bf16[2,14,40,128]{3,2,1,0:T(8,128)(2,1)}, bf16[2,14,40,128]{3,2,1,0:T(8,128)(2,1)S(1)}, u32[]{:S(2)}) copy-start(bf16[2,14,40,128]{3,2,1,0:T(8,128)(2,1)S(1)} %collective-permute-done.10.refs_12_) | copy-start | bytes 860164
  25.0 5.1 %collective-permute-start.12 = (bf16[2,14,40,128]{3,2,1,0:T(8,128)(2,1)S(1)}, bf16[2,14,40,128]{3,2,1,0:T(8,128)(2,1)}, u32[]{:S(2)}, u32[]{:S(2)}) collective-permute-start(bf16[2,14,40,128]{3,2,1,0:T(8,128)(2,1)S(1)} %collective-permute-done.10.refs_12_), channel_id=1, source_target_pairs={{0,1},{1,0},{2,3},{3,2},{4,5},{5,4},{6,7},{7,6},{8,9},{9,8},{10,11... | collective-permute-start | bytes 860168 | tf_op jit(solution)/shard_map/ppermute | solution.py:690
  27.4 2.9 %collective-permute-start.13 = (bf16[2,14,40,128]{3,2,1,0:T(8,128)(2,1)S(1)}, bf16[2,14,40,128]{3,2,1,0:T(8,128)(2,1)}, u32[]{:S(2)}, u32[]{:S(2)}) collective-permute-start(bf16[2,14,40,128]{3,2,1,0:T(8,128)(2,1)S(1)} %collective-permute-done.11.refs_13_), channel_id=1, source_target_pairs={{0,1},{1,0},{2,3},{3,2},{4,5},{5,4},{6,7},{7,6},{8,9},{9,8},{10,11... | collective-permute-start | bytes 860168 | tf_op jit(solution)/shard_map/ppermute | solution.py:690
  39.9 8.8 %copy-start.9 = (s32[1,2,8]{2,1,0:T(2,128)S(1)}, s32[1,2,8]{2,1,0:T(2,128)}, u32[]{:S(2)}) copy-start(s32[1,2,8]{2,1,0:T(2,128)} %param.7) | copy-start | bytes 196
  40.0 8.8 %copy-start.10 = (s32[1,2,8]{2,1,0:T(2,128)S(1)}, s32[1,2,8]{2,1,0:T(2,128)}, u32[]{:S(2)}) copy-start(s32[1,2,8]{2,1,0:T(2,128)} %param.6) | copy-start | bytes 196
  40.0 28.5 %all-to-all-start = ((bf16[8,14,40,128]{3,2,1,0:T(8,128)(2,1)}), bf16[8,14,40,128]{3,2,1,0:T(8,128)(2,1)}, u32[]{:S(2)}, u32[]{:S(2)}) async-start(bf16[8,14,40,128]{3,2,1,0:T(8,128)(2,1)} %get-tuple-element.13), calls=%async_computation | async-start | bytes 2293760 | tf_op jit(solution)/shard_map/all_to_all | solution.py:715
  44.5 23.9 %collective-permute-start.16 = (bf16[4,14,40,128]{3,2,1,0:T(8,128)(2,1)S(1)}, bf16[4,14,40,128]{3,2,1,0:T(8,128)(2,1)S(1)}, u32[]{:S(2)}, u32[]{:S(2)}) collective-permute-start(bf16[4,14,40,128]{3,2,1,0:T(8,128)(2,1)S(1)} %copy-done.11), channel_id=1, source_target_pairs={{24,0},{0,8},{8,16},{16,24},{25,1},{1,9},{9,17},{17,25},{26,2},{2,... | collective-permute-start | bytes 1720328 | tf_op jit(solution)/shard_map/ppermute | solution.py:678
  (6 other events, 13.5 us)
where the time goes:
time: 74.7 us; the launch traced here: 73.2 us
  Pallas kernels  33.3 us (45%)
  starting transfers between devices  28.5 us (38%)
  waiting for transfers between devices  7.04 us (9%)
  local copies, waits for them, and re-layouts  3.41 us (5%)
  other arithmetic  0.78 us (1%)
    pallas_call x1, Pallas kernels, group_pairs(): pl.pallas_call(functools.partial(group_body, orbs, count, grid_cells), ou...  19.7 us
    ppermute x14, starting transfers between devices, group_exchange(): known[k ^ bit] = lax.ppermute(known[k], 'orb', route)  19.4 us
    pallas_call x1, Pallas kernels, forward_pairs(): pl.pallas_call(functools.partial(forward_body, orbs, count, grid_cells),...  9.55 us
    ppermute x3, waiting for transfers between devices, along_space(): lax.ppermute(block, 'space', [((i - distance) % size, i) for i in range(s...  5.48 us
    ppermute x3, starting transfers between devices, along_space(): lax.ppermute(block, 'space', [((i - distance) % size, i) for i in range(s...  4.6 us
    all_to_all x1, starting transfers between devices, per_device(): near = lax.all_to_all(near, 'orb', split_axis=0, concat_axis=0, tiled=True)  4.55 us
    pallas_call x1, Pallas kernels, finish(): pl.pallas_call(functools.partial(finish_body, count, slots), out_shape=ja...  3.5 us
    unnamed x25, local copies, waits for them, and re-layouts  3.13 us
  transfers between devices with their start and end apart: 18, of which 4 were waited for; matrix products, arithmetic and copies ran while one was open for 1% of the time, Pallas kernels for 27%

commit v1 on v0

--- a/solution.py
+++ b/solution.py
@@ -37,7 +37,19 @@
     return pieces
 
 
-def pack_body(box_ref, table_ref, first_ref, second_ref, stage):
+def index_table(refs):
+    free = LANES - USED
+    rows = []
+    for ref in refs:
+        entries = ref[0].astype(jnp.float32)
+        for g in range(2):
+            for start in range(0, entries.shape[1], free):
+                part = entries[g : g + 1, start : start + free]
+                rows.append(jnp.concatenate([jnp.zeros((1, USED), jnp.float32), part], axis=1))
+    return jnp.concatenate(rows + [jnp.zeros((B - len(rows), LANES), jnp.float32)], axis=0)
+
+
+def pack_body(box_ref, send_ref, left_ref, first_ref, second_ref, stage):
     count = box_ref.shape[0]
     lane = lanes_of((B, LANES))
     for n in range(count):
@@ -61,38 +73,49 @@
             keep = (lane >= first) & (lane < last)
             tiles[b % TILES] = jnp.where(keep, moved, tiles[b % TILES])
         if n == 0:
-            tiles[0] = tiles[0] + table_ref[...]
+            tiles[0] = tiles[0] + index_table((send_ref, left_ref))
         out_ref = first_ref if n < count // 2 else second_ref
         for t in range(TILES):
             out_ref[n % (count // 2), t] = tiles[t].astype(out_ref.dtype)
 
 
-def pack(orbitals, table):
+def pack(orbitals, send_index, pair_left):
     count = orbitals.shape[0]
     return pl.pallas_call(
         pack_body,
         out_shape=[jax.ShapeDtypeStruct((count // 2, TILES, B, LANES), jnp.bfloat16)] * 2,
-        in_specs=[pl.BlockSpec(memory_space=pltpu.VMEM)] * 2,
+        in_specs=[pl.BlockSpec(memory_space=pltpu.VMEM)] * 3,
         out_specs=[pl.BlockSpec(memory_space=pltpu.VMEM)] * 2,
         scratch_shapes=[pltpu.VMEM((-(-B * B // LANES), B, LANES), jnp.float32)],
         compiler_params=pltpu.CompilerParams(vmem_limit_bytes=VMEM_BYTES),
         name="pack",
-    )(orbitals, table)
-
-
-def finish_body(count, slots, field_ref, near_ref, far_ref, row_ref, out_ref, total, stage):
-    lane = lanes_of((B, LANES))
+    )(orbitals, send_index, pair_left)
+
+
+def finish_body(field_ref, near_ref, far_ref, row_ref, out_ref, total, near, far, made, stage, *sems):
+    count, slots = field_ref.shape[0], near_ref.shape[0]
+    field_sem, near_sem, far_sem, out_sem = sems
+
+    def copy(source, target, sem):
+        made = pltpu.make_async_copy(source, target, sem)
+        made.start()
+        return made
+
+    fields = [copy(field_ref.at[n], total.at[n], field_sem.at[n]) for n in range(count)]
+    fars = [copy(far_ref.at[n], far.at[n], far_sem.at[n]) for n in range(count)]
+    nears = [copy(near_ref.at[j], near.at[j], near_sem.at[j]) for j in range(slots)]
     for n in range(count):
+        fields[n].wait()
+        fars[n].wait()
         for t in range(TILES):
-            total[n, t] = field_ref[n, t] + far_ref[n, t].astype(jnp.float32)
-
-    def add(j, carry):
+            total[n, t] += far[n, t].astype(jnp.float32)
+    for j in range(slots):
+        nears[j].wait()
         row = row_ref[j]
         for t in range(TILES):
-            total[row, t] += near_ref[j, t].astype(jnp.float32)
-        return carry
-
-    lax.fori_loop(0, slots, add, 0)
+            total[row, t] += near[j, t].astype(jnp.float32)
+    lane = lanes_of((B, LANES))
+    sent = []
     for n in range(count):
         flats = {}
         for b, flat, shift in overlaps():
@@ -106,21 +129,28 @@
             for p in range(PLANES):
                 stage[flat, pl.ds(p, SUB, stride=PLANES), :] = value[p * SUB : p * SUB + SUB]
             width = min(LANES, B * B - flat * LANES)
-            out_ref[n, :, flat * LANES : flat * LANES + width] = stage[flat, :, :width]
+            made[n, :, flat * LANES : flat * LANES + width] = stage[flat, :, :width]
+        sent.append(copy(made.at[n], out_ref.at[n], out_sem.at[n]))
+    for one in sent:
+        one.wait()
 
 
 def finish(field, near, far, rows):
     count, slots = field.shape[0], near.shape[0]
-    vmem = pl.BlockSpec(memory_space=pltpu.VMEM)
+    left = pl.BlockSpec(memory_space=pltpu.HBM)
+    shape = (TILES, B, LANES)
     return pl.pallas_call(
-        functools.partial(finish_body, count, slots),
+        finish_body,
         out_shape=jax.ShapeDtypeStruct((count, B, B * B), jnp.float32),
-        in_specs=[vmem, vmem, vmem, pl.BlockSpec(memory_space=pltpu.SMEM)],
-        out_specs=vmem,
+        in_specs=[left] * 3 + [pl.BlockSpec(memory_space=pltpu.SMEM)],
+        out_specs=left,
         scratch_shapes=[
-            pltpu.VMEM((count, TILES, B, LANES), jnp.float32),
+            pltpu.VMEM((count,) + shape, jnp.float32),
+            pltpu.VMEM((slots,) + shape, near.dtype),
+            pltpu.VMEM((count,) + shape, far.dtype),
+            pltpu.VMEM((count, B, B * B), jnp.float32),
             pltpu.VMEM((-(-B * B // LANES), B, LANES), jnp.float32),
-        ],
+        ] + [pltpu.SemaphoreType.DMA((size,)) for size in (count, slots, count, count)],
         compiler_params=pltpu.CompilerParams(vmem_limit_bytes=VMEM_BYTES),
         name="finish",
     )(field, near, far, rows)
@@ -700,13 +730,7 @@
     group_first = space * orbs * count
     offsets = box_offset.reshape(-1)
 
-    free = LANES - USED
-    entries = jnp.concatenate([send_index[0].reshape(-1), pair_left[0].reshape(-1)])
-    lines = 4 * orbs // free
-    table = jnp.pad(
-        entries.astype(jnp.float32).reshape(lines, free), ((0, B - lines), (USED, 0))
-    )
-    packed = pack(orbitals, table)
+    packed = pack(orbitals, send_index, pair_left)
 
     incoming = [along_space(half, -1) for half in packed]
     pieces = group_exchange(packed, orbs)

time: 74.7 us -> 72.7 us (0.973)
  the two profiles are of different devices: /device:TPU:25 before, /device:TPU:23 now
where the time goes in v1:
time: 72.7 us; the launch traced here: 71.6 us
  Pallas kernels  29.6 us (41%)
  starting transfers between devices  26.5 us (36%)
  waiting for transfers between devices  9.94 us (14%)
  local copies, waits for them, and re-layouts  5.42 us (7%)
    pallas_call x1, Pallas kernels, group_pairs(): pl.pallas_call(functools.partial(group_body, orbs, count, grid_cells), ou...  17.5 us
    ppermute x14, starting transfers between devices, group_exchange(): known[k ^ bit] = lax.ppermute(known[k], 'orb', route)  13.3 us
    ppermute x3, waiting for transfers between devices, along_space(): lax.ppermute(block, 'space', [((i - distance) % size, i) for i in range(s...  7.65 us
    all_to_all x1, starting transfers between devices, per_device(): near = lax.all_to_all(near, 'orb', split_axis=0, concat_axis=0, tiled=True)  7 us
    pallas_call x1, Pallas kernels, forward_pairs(): pl.pallas_call(functools.partial(forward_body, orbs, count, grid_cells),...  6.86 us
    ppermute x3, starting transfers between devices, along_space(): lax.ppermute(block, 'space', [((i - distance) % size, i) for i in range(s...  6.21 us
    unnamed x29, local copies, waits for them, and re-layouts  5.21 us
    pallas_call x1, Pallas kernels, finish(): pl.pallas_call(finish_body, out_shape=jax.ShapeDtypeStruct((count, B, B *...  4.64 us
  transfers between devices with their start and end apart: 18, of which 4 were waited for; matrix products, arithmetic and copies ran while one was open for 2% of the time, Pallas kernels for 24%

profile of v1, /device:TPU:23, one launch (start us, length us, event | category | flops | bytes accessed | tf_op | source)
XLA Modules:
  0.0 71.6 jit_solution(1868229910169377979)
XLA Ops:
  0.0 1.0 %copy-done.1 = bf16[4,40,1600]{2,1,0:T(8,128)(2,1)S(1)} copy-done((bf16[4,40,1600]{2,1,0:T(8,128)(2,1)S(1)}, bf16[4,40,1600]{2,1,0:T(8,128)(2,1)}, u32[]{:S(2)}) %copy-start.1) | copy-done | bytes 512024
  1.0 0.7 copy-done.2
  1.7 0.7 copy-done.4
  2.4 0.6 pack.1
  3.4 0.3 collective-permute-start.2
  3.7 1.5 %collective-permute-start = (bf16[2,14,40,128]{3,2,1,0:T(8,128)(2,1)S(1)}, bf16[2,14,40,128]{3,2,1,0:T(8,128)(2,1)S(1)}, u32[]{:S(2)}, u32[]{:S(2)}) collective-permute-start(bf16[2,14,40,128]{3,2,1,0:T(8,128)(2,1)S(1)} %get-tuple-element.10.refs_0_), channel_id=1, source_target_pairs={{0,1},{1,0},{2,3},{3,2},{4,5},{5,4},{6,7},{7,6},{8,9},{9,8},{10,11... | collective-permute-start | bytes 860168 | tf_op jit(solution)/shard_map/ppermute | solution.py:720
  5.2 5.5 %collective-permute-done.14.refs_16_ = bf16[2,14,40,128]{3,2,1,0:T(8,128)(2,1)S(1)} collective-permute-done((bf16[2,14,40,128]{3,2,1,0:T(8,128)(2,1)S(1)}, bf16[2,14,40,128]{3,2,1,0:T(8,128)(2,1)S(1)}, u32[]{:S(2)}, u32[]{:S(2)}) %collective-permute-start.14) | collective-permute-done | bytes 286752 | tf_op jit(solution)/shard_map/ppermute | solution.py:708
  11.0 0.5 copy-done.11
  11.5 0.3 collective-permute-start.3
  11.7 3.0 %collective-permute-start.1 = (bf16[2,14,40,128]{3,2,1,0:T(8,128)(2,1)S(1)}, bf16[2,14,40,128]{3,2,1,0:T(8,128)(2,1)S(1)}, u32[]{:S(2)}, u32[]{:S(2)}) collective-permute-start(bf16[2,14,40,128]{3,2,1,0:T(8,128)(2,1)S(1)} %get-tuple-element.11.refs_1_), channel_id=1, source_target_pairs={{0,1},{1,0},{2,3},{3,2},{4,5},{5,4},{6,7},{7,6},{8,9},{9,8},{10,11... | collective-permute-start | bytes 860168 | tf_op jit(solution)/shard_map/ppermute | solution.py:720
  14.8 2.1 %collective-permute-done.15.refs_17_ = bf16[2,14,40,128]{3,2,1,0:T(8,128)(2,1)S(1)} collective-permute-done((bf16[2,14,40,128]{3,2,1,0:T(8,128)(2,1)S(1)}, bf16[2,14,40,128]{3,2,1,0:T(8,128)(2,1)S(1)}, u32[]{:S(2)}, u32[]{:S(2)}) %collective-permute-start.15) | collective-permute-done | bytes 286752 | tf_op jit(solution)/shard_map/ppermute | solution.py:708
  17.1 0.3 collective-permute-start.11
  17.6 3.7 %collective-permute-start.4 = (bf16[2,14,40,128]{3,2,1,0:T(8,128)(2,1)S(1)}, bf16[2,14,40,128]{3,2,1,0:T(8,128)(2,1)S(1)}, u32[]{:S(2)}, u32[]{:S(2)}) collective-permute-start(bf16[2,14,40,128]{3,2,1,0:T(8,128)(2,1)S(1)} %collective-permute-done.2.refs_4_), channel_id=1, source_target_pairs={{0,1},{1,0},{2,3},{3,2},{4,5},{5,4},{6,7},{7,6},{8,9},{9,8},{10,11... | collective-permute-start | bytes 860168 | tf_op jit(solution)/shard_map/ppermute | solution.py:720
  21.3 0.5 collective-permute-start.5
  21.8 2.0 %collective-permute-done.10.refs_12_ = bf16[2,14,40,128]{3,2,1,0:T(8,128)(2,1)S(1)} collective-permute-done((bf16[2,14,40,128]{3,2,1,0:T(8,128)(2,1)S(1)}, bf16[2,14,40,128]{3,2,1,0:T(8,128)(2,1)S(1)}, u32[]{:S(2)}, u32[]{:S(2)}) %collective-permute-start.10) | collective-permute-done | bytes 286752 | tf_op jit(solution)/shard_map/ppermute | solution.py:720
  23.8 2.4 %collective-permute-start.12 = (bf16[2,14,40,128]{3,2,1,0:T(8,128)(2,1)S(1)}, bf16[2,14,40,128]{3,2,1,0:T(8,128)(2,1)}, u32[]{:S(2)}, u32[]{:S(2)}) collective-permute-start(bf16[2,14,40,128]{3,2,1,0:T(8,128)(2,1)S(1)} %collective-permute-done.10.refs_12_), channel_id=1, source_target_pairs={{0,1},{1,0},{2,3},{3,2},{4,5},{5,4},{6,7},{7,6},{8,9},{9,8},{10,11... | collective-permute-start | bytes 860168 | tf_op jit(solution)/shard_map/ppermute | solution.py:720
  26.2 0.7 collective-permute-start.13
  26.9 0.8 %copy.5 = s32[128,3]{1,0:T(8,128)S(1)} copy(s32[128,3]{0,1:T(4,128)} %param.5) | data formatting | bytes 3072 | tf_op args[1]
  28.3 6.9 %forward_pairs.1 = (bf16[8,14,40,128]{3,2,1,0:T(8,128)(2,1)}, bf16[4,14,40,128]{3,2,1,0:T(8,128)(2,1)}, s32[32]{0:T(128)S(1)}) custom-call(s32[3]{0:T(128)S(1)} %pad_add_fusion.where_ref, s32[384]{0:T(512)S(1)} %reshape.3.offset_ref, bf16[2,14,40,128]{3,2,1,0:T(8,128)(2,1)S(1)} %get-tuple-element.10.refs_0_, ...), custom_call_target="tpu_custom_call" | custom-call | tf_op jit(solution)/shard_map/forward_pairs/pallas_call | solution.py:586
  35.2 7.0 %all-to-all-start = ((bf16[8,14,40,128]{3,2,1,0:T(8,128)(2,1)}), bf16[8,14,40,128]{3,2,1,0:T(8,128)(2,1)}, u32[]{:S(2)}, u32[]{:S(2)}) async-start(bf16[8,14,40,128]{3,2,1,0:T(8,128)(2,1)} %get-tuple-element.13), calls=%async_computation | async-start | bytes 2293760 | tf_op jit(solution)/shard_map/all_to_all | solution.py:739
  42.2 6.0 %collective-permute-start.16 = (bf16[4,14,40,128]{3,2,1,0:T(8,128)(2,1)S(1)}, bf16[4,14,40,128]{3,2,1,0:T(8,128)(2,1)S(1)}, u32[]{:S(2)}, u32[]{:S(2)}) collective-permute-start(bf16[4,14,40,128]{3,2,1,0:T(8,128)(2,1)S(1)} %copy-done.13), channel_id=1, source_target_pairs={{24,0},{0,8},{8,16},{16,24},{25,1},{1,9},{9,17},{17,25},{26,2},{2,... | collective-permute-start | bytes 1720328 | tf_op jit(solution)/shard_map/ppermute | solution.py:708
  48.2 17.5 %group_pairs.1.field_ref = f32[4,14,40,128]{3,2,1,0:T(8,128)} custom-call(s32[3]{0:T(128)S(1)} %pad_add_fusion.where_ref, s32[384]{0:T(512)S(1)} %reshape.3.offset_ref, s32[8]{0:T(128)S(1)} %get-tuple-element.16.mine_ref, s32[8]{0:T(128)S(1)} %get-tuple-element.17.sent_ref, s32[32]{0:T(128)S(1)} %get-tuple-element.12.index_ref, ...), custom_call_target="tpu_custom_call" | custom-call | tf_op jit(solution)/shard_map/group_pairs/pallas_call | solution.py:692
  65.7 1.2 %copy-done = f32[4,14,40,128]{3,2,1,0:T(8,128)S(1)} copy-done((f32[4,14,40,128]{3,2,1,0:T(8,128)S(1)}, f32[4,14,40,128]{3,2,1,0:T(8,128)}, u32[]{:S(2)}) %copy-start) | copy-done | bytes 1146904
  67.0 4.6 %finish.1 = f32[4,40,1600]{2,1,0:T(8,128)} custom-call(f32[4,14,40,128]{3,2,1,0:T(8,128)S(1)} %copy-done, bf16[8,14,40,128]{3,2,1,0:T(8,128)(2,1)} %all-to-all-done.near_ref, bf16[4,14,40,128]{3,2,1,0:T(8,128)(2,1)S(1)} %collective-permute-done.16.far_ref, s32[8]{0:T(128)S(1)} %get-tuple-element.15.row_ref), custom_call_target="tpu_custom_call" | custom-call | tf_op jit(solution)/shard_map/finish/pallas_call | solution.py:142
  (48 shorter events, 1.8 us)
Async XLA Ops:
  3.0 7.8 %collective-permute-start.14 = (bf16[2,14,40,128]{3,2,1,0:T(8,128)(2,1)S(1)}, bf16[2,14,40,128]{3,2,1,0:T(8,128)(2,1)S(1)}, u32[]{:S(2)}, u32[]{:S(2)}) collective-permute-start(bf16[2,14,40,128]{3,2,1,0:T(8,128)(2,1)S(1)} %get-tuple-element.10.refs_0_), channel_id=1, source_target_pairs={{8,0},{16,8},{24,16},{0,24},{9,1},{17,9},{25,17},{1,25},{10,2},{18... | collective-permute-start | bytes 860168 | tf_op jit(solution)/shard_map/ppermute | solution.py:708
  3.2 8.2 %collective-permute-start.6 = (bf16[2,14,40,128]{3,2,1,0:T(8,128)(2,1)S(1)}, bf16[2,14,40,128]{3,2,1,0:T(8,128)(2,1)S(1)}, u32[]{:S(2)}, u32[]{:S(2)}) collective-permute-start(bf16[2,14,40,128]{3,2,1,0:T(8,128)(2,1)S(1)} %get-tuple-element.10.refs_0_), channel_id=1, source_target_pairs={{0,4},{1,5},{2,6},{3,7},{4,0},{5,1},{6,2},{7,3},{8,12},{9,13},{10,... | collective-permute-start | bytes 860168 | tf_op jit(solution)/shard_map/ppermute | solution.py:720
  3.4 8.3 %collective-permute-start.2 = (bf16[2,14,40,128]{3,2,1,0:T(8,128)(2,1)S(1)}, bf16[2,14,40,128]{3,2,1,0:T(8,128)(2,1)S(1)}, u32[]{:S(2)}, u32[]{:S(2)}) collective-permute-start(bf16[2,14,40,128]{3,2,1,0:T(8,128)(2,1)S(1)} %get-tuple-element.10.refs_0_), channel_id=1, source_target_pairs={{0,2},{1,3},{2,0},{3,1},{4,6},{5,7},{6,4},{7,5},{8,10},{9,11},{10,... | collective-permute-start | bytes 860168 | tf_op jit(solution)/shard_map/ppermute | solution.py:720
  3.7 11.0 %collective-permute-start = (bf16[2,14,40,128]{3,2,1,0:T(8,128)(2,1)S(1)}, bf16[2,14,40,128]{3,2,1,0:T(8,128)(2,1)S(1)}, u32[]{:S(2)}, u32[]{:S(2)}) collective-permute-start(bf16[2,14,40,128]{3,2,1,0:T(8,128)(2,1)S(1)} %get-tuple-element.10.refs_0_), channel_id=1, source_target_pairs={{0,1},{1,0},{2,3},{3,2},{4,5},{5,4},{6,7},{7,6},{8,9},{9,8},{10,11... | collective-permute-start | bytes 860168 | tf_op jit(solution)/shard_map/ppermute | solution.py:720
  5.2 11.7 %collective-permute-start.15 = (bf16[2,14,40,128]{3,2,1,0:T(8,128)(2,1)S(1)}, bf16[2,14,40,128]{3,2,1,0:T(8,128)(2,1)S(1)}, u32[]{:S(2)}, u32[]{:S(2)}) collective-permute-start(bf16[2,14,40,128]{3,2,1,0:T(8,128)(2,1)S(1)} %get-tuple-element.11.refs_1_), channel_id=1, source_target_pairs={{8,0},{16,8},{24,16},{0,24},{9,1},{17,9},{25,17},{1,25},{10,2},{18... | collective-permute-start | bytes 860168 | tf_op jit(solution)/shard_map/ppermute | solution.py:708
  10.7 6.4 %collective-permute-start.7 = (bf16[2,14,40,128]{3,2,1,0:T(8,128)(2,1)S(1)}, bf16[2,14,40,128]{3,2,1,0:T(8,128)(2,1)S(1)}, u32[]{:S(2)}, u32[]{:S(2)}) collective-permute-start(bf16[2,14,40,128]{3,2,1,0:T(8,128)(2,1)S(1)} %get-tuple-element.11.refs_1_), channel_id=1, source_target_pairs={{0,4},{1,5},{2,6},{3,7},{4,0},{5,1},{6,2},{7,3},{8,12},{9,13},{10,... | collective-permute-start | bytes 860168 | tf_op jit(solution)/shard_map/ppermute | solution.py:720
  11.5 16.8 %copy-start.6 = (bf16[2,14,40,128]{3,2,1,0:T(8,128)(2,1)}, bf16[2,14,40,128]{3,2,1,0:T(8,128)(2,1)S(1)}, u32[]{:S(2)}) copy-start(bf16[2,14,40,128]{3,2,1,0:T(8,128)(2,1)S(1)} %collective-permute-done.6.refs_8_) | copy-start | bytes 860164
  11.5 6.2 %collective-permute-start.3 = (bf16[2,14,40,128]{3,2,1,0:T(8,128)(2,1)S(1)}, bf16[2,14,40,128]{3,2,1,0:T(8,128)(2,1)S(1)}, u32[]{:S(2)}, u32[]{:S(2)}) collective-permute-start(bf16[2,14,40,128]{3,2,1,0:T(8,128)(2,1)S(1)} %get-tuple-element.11.refs_1_), channel_id=1, source_target_pairs={{0,2},{1,3},{2,0},{3,1},{4,6},{5,7},{6,4},{7,5},{8,10},{9,11},{10,... | collective-permute-start | bytes 860168 | tf_op jit(solution)/shard_map/ppermute | solution.py:720
  11.7 9.6 %collective-permute-start.1 = (bf16[2,14,40,128]{3,2,1,0:T(8,128)(2,1)S(1)}, bf16[2,14,40,128]{3,2,1,0:T(8,128)(2,1)S(1)}, u32[]{:S(2)}, u32[]{:S(2)}) collective-permute-start(bf16[2,14,40,128]{3,2,1,0:T(8,128)(2,1)S(1)} %get-tuple-element.11.refs_1_), channel_id=1, source_target_pairs={{0,1},{1,0},{2,3},{3,2},{4,5},{5,4},{6,7},{7,6},{8,9},{9,8},{10,11... | collective-permute-start | bytes 860168 | tf_op jit(solution)/shard_map/ppermute | solution.py:720
  14.7 6.6 %collective-permute-start.8 = (bf16[2,14,40,128]{3,2,1,0:T(8,128)(2,1)S(1)}, bf16[2,14,40,128]{3,2,1,0:T(8,128)(2,1)S(1)}, u32[]{:S(2)}, u32[]{:S(2)}) collective-permute-start(bf16[2,14,40,128]{3,2,1,0:T(8,128)(2,1)S(1)} %collective-permute-done.6.refs_8_), channel_id=1, source_target_pairs={{0,1},{1,0},{2,3},{3,2},{4,5},{5,4},{6,7},{7,6},{8,9},{9,8},{10,11... | collective-permute-start | bytes 860168 | tf_op jit(solution)/shard_map/ppermute | solution.py:720
  16.9 6.9 %collective-permute-start.10 = (bf16[2,14,40,128]{3,2,1,0:T(8,128)(2,1)S(1)}, bf16[2,14,40,128]{3,2,1,0:T(8,128)(2,1)S(1)}, u32[]{:S(2)}, u32[]{:S(2)}) collective-permute-start(bf16[2,14,40,128]{3,2,1,0:T(8,128)(2,1)S(1)} %collective-permute-done.2.refs_4_), channel_id=1, source_target_pairs={{0,4},{1,5},{2,6},{3,7},{4,0},{5,1},{6,2},{7,3},{8,12},{9,13},{10,... | collective-permute-start | bytes 860168 | tf_op jit(solution)/shard_map/ppermute | solution.py:720
  17.1 11.2 %copy-start.7 = (bf16[2,14,40,128]{3,2,1,0:T(8,128)(2,1)}, bf16[2,14,40,128]{3,2,1,0:T(8,128)(2,1)S(1)}, u32[]{:S(2)}) copy-start(bf16[2,14,40,128]{3,2,1,0:T(8,128)(2,1)S(1)} %collective-permute-done.7.refs_9_) | copy-start | bytes 860164
  17.1 9.1 %collective-permute-start.11 = (bf16[2,14,40,128]{3,2,1,0:T(8,128)(2,1)S(1)}, bf16[2,14,40,128]{3,2,1,0:T(8,128)(2,1)S(1)}, u32[]{:S(2)}, u32[]{:S(2)}) collective-permute-start(bf16[2,14,40,128]{3,2,1,0:T(8,128)(2,1)S(1)} %collective-permute-done.7.refs_9_), channel_id=1, source_target_pairs={{0,2},{1,3},{2,0},{3,1},{4,6},{5,7},{6,4},{7,5},{8,10},{9,11},{10,... | collective-permute-start | bytes 860168 | tf_op jit(solution)/shard_map/ppermute | solution.py:720
  17.6 10.4 %collective-permute-start.4 = (bf16[2,14,40,128]{3,2,1,0:T(8,128)(2,1)S(1)}, bf16[2,14,40,128]{3,2,1,0:T(8,128)(2,1)S(1)}, u32[]{:S(2)}, u32[]{:S(2)}) collective-permute-start(bf16[2,14,40,128]{3,2,1,0:T(8,128)(2,1)S(1)} %collective-permute-done.2.refs_4_), channel_id=1, source_target_pairs={{0,1},{1,0},{2,3},{3,2},{4,5},{5,4},{6,7},{7,6},{8,9},{9,8},{10,11... | collective-permute-start | bytes 860168 | tf_op jit(solution)/shard_map/ppermute | solution.py:720
  21.3 6.7 %collective-permute-start.9 = (bf16[2,14,40,128]{3,2,1,0:T(8,128)(2,1)S(1)}, bf16[2,14,40,128]{3,2,1,0:T(8,128)(2,1)}, u32[]{:S(2)}, u32[]{:S(2)}) collective-permute-start(bf16[2,14,40,128]{3,2,1,0:T(8,128)(2,1)S(1)} %collective-permute-done.7.refs_9_), channel_id=1, source_target_pairs={{0,1},{1,0},{2,3},{3,2},{4,5},{5,4},{6,7},{7,6},{8,9},{9,8},{10,11... | collective-permute-start | bytes 860168 | tf_op jit(solution)/shard_map/ppermute | solution.py:720
  21.3 7.0 %copy-start.8 = (bf16[2,14,40,128]{3,2,1,0:T(8,128)(2,1)}, bf16[2,14,40,128]{3,2,1,0:T(8,128)(2,1)S(1)}, u32[]{:S(2)}) copy-start(bf16[2,14,40,128]{3,2,1,0:T(8,128)(2,1)S(1)} %collective-permute-done.8.refs_10_) | copy-start | bytes 860164
  21.3 6.7 %collective-permute-start.5 = (bf16[2,14,40,128]{3,2,1,0:T(8,128)(2,1)S(1)}, bf16[2,14,40,128]{3,2,1,0:T(8,128)(2,1)}, u32[]{:S(2)}, u32[]{:S(2)}) collective-permute-start(bf16[2,14,40,128]{3,2,1,0:T(8,128)(2,1)S(1)} %collective-permute-done.3.refs_5_), channel_id=1, source_target_pairs={{0,1},{1,0},{2,3},{3,2},{4,5},{5,4},{6,7},{7,6},{8,9},{9,8},{10,11... | collective-permute-start | bytes 860168 | tf_op jit(solution)/shard_map/ppermute | solution.py:720
  23.8 4.2 %collective-permute-start.12 = (bf16[2,14,40,128]{3,2,1,0:T(8,128)(2,1)S(1)}, bf16[2,14,40,128]{3,2,1,0:T(8,128)(2,1)}, u32[]{:S(2)}, u32[]{:S(2)}) collective-permute-start(bf16[2,14,40,128]{3,2,1,0:T(8,128)(2,1)S(1)} %collective-permute-done.10.refs_12_), channel_id=1, source_target_pairs={{0,1},{1,0},{2,3},{3,2},{4,5},{5,4},{6,7},{7,6},{8,9},{9,8},{10,11... | collective-permute-start | bytes 860168 | tf_op jit(solution)/shard_map/ppermute | solution.py:720
  26.2 2.0 %collective-permute-start.13 = (bf16[2,14,40,128]{3,2,1,0:T(8,128)(2,1)S(1)}, bf16[2,14,40,128]{3,2,1,0:T(8,128)(2,1)}, u32[]{:S(2)}, u32[]{:S(2)}) collective-permute-start(bf16[2,14,40,128]{3,2,1,0:T(8,128)(2,1)S(1)} %collective-permute-done.11.refs_13_), channel_id=1, source_target_pairs={{0,1},{1,0},{2,3},{3,2},{4,5},{5,4},{6,7},{7,6},{8,9},{9,8},{10,11... | collective-permute-start | bytes 860168 | tf_op jit(solution)/shard_map/ppermute | solution.py:720
  35.2 7.0 %copy-start.13 = (bf16[4,14,40,128]{3,2,1,0:T(8,128)(2,1)S(1)}, bf16[4,14,40,128]{3,2,1,0:T(8,128)(2,1)}, u32[]{:S(2)}) copy-start(bf16[4,14,40,128]{3,2,1,0:T(8,128)(2,1)} %get-tuple-element.14) | copy-start | bytes 1720324
  35.2 13.0 %copy-start.3 = (s32[1,2,8]{2,1,0:T(2,128)S(1)}, s32[1,2,8]{2,1,0:T(2,128)}, u32[]{:S(2)}) copy-start(s32[1,2,8]{2,1,0:T(2,128)} %left_ref.1) | copy-start | bytes 196
  35.2 13.0 %copy-start.5 = (s32[1,2,8]{2,1,0:T(2,128)S(1)}, s32[1,2,8]{2,1,0:T(2,128)}, u32[]{:S(2)}) copy-start(s32[1,2,8]{2,1,0:T(2,128)} %send_ref.1) | copy-start | bytes 196
  35.2 30.5 %all-to-all-start = ((bf16[8,14,40,128]{3,2,1,0:T(8,128)(2,1)}), bf16[8,14,40,128]{3,2,1,0:T(8,128)(2,1)}, u32[]{:S(2)}, u32[]{:S(2)}) async-start(bf16[8,14,40,128]{3,2,1,0:T(8,128)(2,1)} %get-tuple-element.13), calls=%async_computation | async-start | bytes 2293760 | tf_op jit(solution)/shard_map/all_to_all | solution.py:739
  42.2 23.5 %collective-permute-start.16 = (bf16[4,14,40,128]{3,2,1,0:T(8,128)(2,1)S(1)}, bf16[4,14,40,128]{3,2,1,0:T(8,128)(2,1)S(1)}, u32[]{:S(2)}, u32[]{:S(2)}) collective-permute-start(bf16[4,14,40,128]{3,2,1,0:T(8,128)(2,1)S(1)} %copy-done.13), channel_id=1, source_target_pairs={{24,0},{0,8},{8,16},{16,24},{25,1},{1,9},{9,17},{17,25},{26,2},{2,... | collective-permute-start | bytes 1720328 | tf_op jit(solution)/shard_map/ppermute | solution.py:708
  (8 other events, 11.6 us)

commit v2 on v0

--- a/solution.py
+++ b/solution.py
@@ -37,7 +37,7 @@
     return pieces
 
 
-def pack_body(box_ref, table_ref, first_ref, second_ref, stage):
+def pack_body(box_ref, table_ref, whole_ref, first_ref, second_ref, stage):
     count = box_ref.shape[0]
     lane = lanes_of((B, LANES))
     for n in range(count):
@@ -64,16 +64,21 @@
             tiles[0] = tiles[0] + table_ref[...]
         out_ref = first_ref if n < count // 2 else second_ref
         for t in range(TILES):
-            out_ref[n % (count // 2), t] = tiles[t].astype(out_ref.dtype)
+            value = tiles[t].astype(out_ref.dtype)
+            whole_ref[n, t] = value
+            out_ref[n % (count // 2), t] = value
 
 
 def pack(orbitals, table):
     count = orbitals.shape[0]
     return pl.pallas_call(
         pack_body,
-        out_shape=[jax.ShapeDtypeStruct((count // 2, TILES, B, LANES), jnp.bfloat16)] * 2,
+        out_shape=[
+            jax.ShapeDtypeStruct((size, TILES, B, LANES), jnp.bfloat16)
+            for size in (count, count // 2, count // 2)
+        ],
         in_specs=[pl.BlockSpec(memory_space=pltpu.VMEM)] * 2,
-        out_specs=[pl.BlockSpec(memory_space=pltpu.VMEM)] * 2,
+        out_specs=[pl.BlockSpec(memory_space=pltpu.VMEM)] * 3,
         scratch_shapes=[pltpu.VMEM((-(-B * B // LANES), B, LANES), jnp.float32)],
         compiler_params=pltpu.CompilerParams(vmem_limit_bytes=VMEM_BYTES),
         name="pack",
@@ -460,25 +465,24 @@
 
 def forward_body(orbs, count, grid_cells, where_ref, offset_ref, *refs):
     pieces = [refs[2 * k : 2 * k + 2] for k in range(orbs)]
-    incoming = refs[2 * orbs : 2 * orbs + 2]
+    incoming = refs[2 * orbs]
     near_ref, far_ref, index_ref, meta, held, far_sum, meta_sem, box_sem, listed = refs[
-        2 * orbs + 2 : 2 * orbs + 11
+        2 * orbs + 1 : 2 * orbs + 10
     ]
-    scratch = refs[2 * orbs + 11 :]
+    scratch = refs[2 * orbs + 10 :]
     batch = listed.shape[0] // FIELDS
-    part = count // 2
     me = where_ref[2]
     first_left, first_right = where_ref[0], where_ref[1]
 
     tables = [
         pltpu.make_async_copy(source[0].at[0, 0], meta.at[k], meta_sem.at[k])
-        for k, source in enumerate(pieces + [incoming])
+        for k, source in enumerate(pieces + [[incoming]])
     ]
     for copy in tables:
         copy.start()
     rights = [
         pltpu.make_async_copy(
-            incoming[n // part].at[n % part], held.at[orbs + n], box_sem.at[orbs + n]
+            incoming.at[n], held.at[orbs + n], box_sem.at[orbs + n]
         )
         for n in range(count)
     ]
@@ -560,7 +564,7 @@
             jax.ShapeDtypeStruct((count,) + shape, jnp.bfloat16),
             jax.ShapeDtypeStruct((4 * orbs,), jnp.int32),
         ),
-        in_specs=[smem] * 2 + [left] * (2 * orbs + 2),
+        in_specs=[smem] * 2 + [left] * (2 * orbs + 1),
         out_specs=(vmem, vmem, smem),
         scratch_shapes=[
             pltpu.VMEM((orbs + 1, B, LANES), jnp.bfloat16),
@@ -571,7 +575,7 @@
         ] + slot_scratch(8),
         compiler_params=pltpu.CompilerParams(vmem_limit_bytes=VMEM_BYTES),
         name="forward_pairs",
-    )(where, offsets, *[half for piece in pieces for half in piece], *incoming)
+    )(where, offsets, *[half for piece in pieces for half in piece], incoming)
 
 
 def group_body(orbs, count, grid_cells, where_ref, offset_ref, mine_ref, sent_ref, index_ref, *refs):
@@ -706,9 +710,9 @@
     table = jnp.pad(
         entries.astype(jnp.float32).reshape(lines, free), ((0, B - lines), (USED, 0))
     )
-    packed = pack(orbitals, table)
-
-    incoming = [along_space(half, -1) for half in packed]
+    whole, *packed = pack(orbitals, table)
+
+    incoming = along_space(whole, -1)
     pieces = group_exchange(packed, orbs)
     where = jnp.stack([group_first, ((space + 1) % spaces * orbs + orb) * count, orb])
     near, far, index = forward_pairs(where, offsets, pieces, incoming, count, grid_cells)

time: 74.7 us -> 73.9 us (0.989)
  the two profiles are of different devices: /device:TPU:25 before, /device:TPU:6 now
where the time goes in v2:
time: 73.9 us; the launch traced here: 73.5 us
  Pallas kernels  33.7 us (46%)
  starting transfers between devices  19.6 us (27%)
  waiting for transfers between devices  16 us (22%)
  local copies, waits for them, and re-layouts  3.39 us (5%)
  other arithmetic  0.78 us (1%)
    pallas_call x1, Pallas kernels, group_pairs(): pl.pallas_call(functools.partial(group_body, orbs, count, grid_cells), ou...  21.6 us
    ppermute x14, waiting for transfers between devices, group_exchange(): known[k ^ bit] = lax.ppermute(known[k], 'orb', route)  15.6 us
    all_to_all x1, starting transfers between devices, per_device(): near = lax.all_to_all(near, 'orb', split_axis=0, concat_axis=0, tiled=True)  8.89 us
    pallas_call x1, Pallas kernels, forward_pairs(): pl.pallas_call(functools.partial(forward_body, orbs, count, grid_cells),...  7.96 us
    ppermute x14, starting transfers between devices, group_exchange(): known[k ^ bit] = lax.ppermute(known[k], 'orb', route)  6.16 us
    ppermute x2, starting transfers between devices, along_space(): lax.ppermute(block, 'space', [((i - distance) % size, i) for i in range(s...  4.59 us
    pallas_call x1, Pallas kernels, finish(): pl.pallas_call(functools.partial(finish_body, count, slots), out_shape=ja...  3.55 us
    unnamed x15, local copies, waits for them, and re-layouts  3.11 us
  transfers between devices with their start and end apart: 17, of which 7 were waited for; matrix products, arithmetic and copies ran while one was open for 1% of the time, Pallas kernels for 29%

profile of v2, /device:TPU:6, one launch (start us, length us, event | category | flops | bytes accessed | tf_op | source)
XLA Modules:
  0.0 73.5 jit_solution(16897130325445495889)
XLA Ops:
  0.0 0.7 add_convert_fusion
  0.8 1.0 %copy-done.1 = bf16[4,40,1600]{2,1,0:T(8,128)(2,1)S(1)} copy-done((bf16[4,40,1600]{2,1,0:T(8,128)(2,1)S(1)}, bf16[4,40,1600]{2,1,0:T(8,128)(2,1)}, u32[]{:S(2)}) %copy-start.1) | copy-done | bytes 512024
  1.8 0.6 pack.1
  2.4 0.6 collective-permute-start.6
  3.1 1.9 %collective-permute-start.7 = (bf16[2,14,40,128]{3,2,1,0:T(8,128)(2,1)S(1)}, bf16[2,14,40,128]{3,2,1,0:T(8,128)(2,1)S(1)}, u32[]{:S(2)}, u32[]{:S(2)}) collective-permute-start(bf16[2,14,40,128]{3,2,1,0:T(8,128)(2,1)S(1)} %get-tuple-element.12.refs_1_), channel_id=1, source_target_pairs={{0,4},{1,5},{2,6},{3,7},{4,0},{5,1},{6,2},{7,3},{8,12},{9,13},{10,... | collective-permute-start | bytes 860168 | tf_op jit(solution)/shard_map/ppermute | solution.py:694
  5.0 1.5 %collective-permute-start.3 = (bf16[2,14,40,128]{3,2,1,0:T(8,128)(2,1)S(1)}, bf16[2,14,40,128]{3,2,1,0:T(8,128)(2,1)S(1)}, u32[]{:S(2)}, u32[]{:S(2)}) collective-permute-start(bf16[2,14,40,128]{3,2,1,0:T(8,128)(2,1)S(1)} %get-tuple-element.12.refs_1_), channel_id=1, source_target_pairs={{0,2},{1,3},{2,0},{3,1},{4,6},{5,7},{6,4},{7,5},{8,10},{9,11},{10,... | collective-permute-start | bytes 860168 | tf_op jit(solution)/shard_map/ppermute | solution.py:694
  6.5 5.7 %collective-permute-done.6.refs_8_ = bf16[2,14,40,128]{3,2,1,0:T(8,128)(2,1)S(1)} collective-permute-done((bf16[2,14,40,128]{3,2,1,0:T(8,128)(2,1)S(1)}, bf16[2,14,40,128]{3,2,1,0:T(8,128)(2,1)S(1)}, u32[]{:S(2)}, u32[]{:S(2)}) %collective-permute-start.6) | collective-permute-done | bytes 286752 | tf_op jit(solution)/shard_map/ppermute | solution.py:694
  12.2 0.5 collective-permute-done.2.refs_4_
  12.7 3.6 %collective-permute-start.14 = (bf16[4,14,40,128]{3,2,1,0:T(8,128)(2,1)S(1)}, bf16[4,14,40,128]{3,2,1,0:T(8,128)(2,1)}, u32[]{:S(2)}, u32[]{:S(2)}) collective-permute-start(bf16[4,14,40,128]{3,2,1,0:T(8,128)(2,1)S(1)} %get-tuple-element.13), channel_id=1, source_target_pairs={{8,0},{16,8},{24,16},{0,24},{9,1},{17,9},{25,17},{1,25},{10,2},{18... | collective-permute-start | bytes 1720328 | tf_op jit(solution)/shard_map/ppermute | solution.py:682
  16.3 0.8 %collective-permute-done.7.refs_9_ = bf16[2,14,40,128]{3,2,1,0:T(8,128)(2,1)S(1)} collective-permute-done((bf16[2,14,40,128]{3,2,1,0:T(8,128)(2,1)S(1)}, bf16[2,14,40,128]{3,2,1,0:T(8,128)(2,1)S(1)}, u32[]{:S(2)}, u32[]{:S(2)}) %collective-permute-start.7) | collective-permute-done | bytes 286752 | tf_op jit(solution)/shard_map/ppermute | solution.py:694
  17.2 0.8 %collective-permute-start.10 = (bf16[2,14,40,128]{3,2,1,0:T(8,128)(2,1)S(1)}, bf16[2,14,40,128]{3,2,1,0:T(8,128)(2,1)}, u32[]{:S(2)}, u32[]{:S(2)}) collective-permute-start(bf16[2,14,40,128]{3,2,1,0:T(8,128)(2,1)S(1)} %collective-permute-done.2.refs_4_), channel_id=1, source_target_pairs={{0,4},{1,5},{2,6},{3,7},{4,0},{5,1},{6,2},{7,3},{8,12},{9,13},{10,... | collective-permute-start | bytes 860168 | tf_op jit(solution)/shard_map/ppermute | solution.py:694
  18.1 0.5 collective-permute-start.11
  18.7 7.0 %collective-permute-done.10.refs_12_ = bf16[2,14,40,128]{3,2,1,0:T(8,128)(2,1)} collective-permute-done((bf16[2,14,40,128]{3,2,1,0:T(8,128)(2,1)S(1)}, bf16[2,14,40,128]{3,2,1,0:T(8,128)(2,1)}, u32[]{:S(2)}, u32[]{:S(2)}) %collective-permute-start.10) | collective-permute-done | bytes 286752 | tf_op jit(solution)/shard_map/ppermute | solution.py:694
  25.7 0.5 collective-permute-start.12
  26.2 1.1 %collective-permute-done.11.refs_13_ = bf16[2,14,40,128]{3,2,1,0:T(8,128)(2,1)} collective-permute-done((bf16[2,14,40,128]{3,2,1,0:T(8,128)(2,1)S(1)}, bf16[2,14,40,128]{3,2,1,0:T(8,128)(2,1)}, u32[]{:S(2)}, u32[]{:S(2)}) %collective-permute-start.11) | collective-permute-done | bytes 286752 | tf_op jit(solution)/shard_map/ppermute | solution.py:694
  27.3 0.8 %copy.5 = s32[128,3]{1,0:T(8,128)S(1)} copy(s32[128,3]{0,1:T(4,128)} %param.5) | data formatting | bytes 3072 | tf_op args[1]
  28.4 0.3 collective-permute-done.14.refs_16_
  28.7 0.5 collective-permute-done.13.refs_15_
  29.2 8.0 %forward_pairs.1 = (bf16[8,14,40,128]{3,2,1,0:T(8,128)(2,1)}, bf16[4,14,40,128]{3,2,1,0:T(8,128)(2,1)}, s32[32]{0:T(128)S(1)}) custom-call(s32[3]{0:T(128)S(1)} %pad_add_fusion.where_ref, s32[384]{0:T(512)S(1)} %reshape.8.offset_ref, bf16[2,14,40,128]{3,2,1,0:T(8,128)(2,1)S(1)} %get-tuple-element.11.refs_0_, ...), custom_call_target="tpu_custom_call" | custom-call | tf_op jit(solution)/shard_map/forward_pairs/pallas_call | solution.py:560
  37.2 8.9 %all-to-all-start = ((bf16[8,14,40,128]{3,2,1,0:T(8,128)(2,1)}), bf16[8,14,40,128]{3,2,1,0:T(8,128)(2,1)}, u32[]{:S(2)}, u32[]{:S(2)}) async-start(bf16[8,14,40,128]{3,2,1,0:T(8,128)(2,1)} %get-tuple-element.15), calls=%async_computation | async-start | bytes 2293760 | tf_op jit(solution)/shard_map/all_to_all | solution.py:719
  46.1 1.0 %collective-permute-start.15 = (bf16[4,14,40,128]{3,2,1,0:T(8,128)(2,1)}, bf16[4,14,40,128]{3,2,1,0:T(8,128)(2,1)S(1)}, u32[]{:S(2)}, u32[]{:S(2)}) collective-permute-start(bf16[4,14,40,128]{3,2,1,0:T(8,128)(2,1)} %get-tuple-element.16), channel_id=1, source_target_pairs={{24,0},{0,8},{8,16},{16,24},{25,1},{1,9},{9,17},{17,25},{26,2},{2,... | collective-permute-start | bytes 1720328 | tf_op jit(solution)/shard_map/ppermute | solution.py:682
  47.1 21.6 %group_pairs.1.field_ref = f32[4,14,40,128]{3,2,1,0:T(8,128)} custom-call(s32[3]{0:T(128)S(1)} %pad_add_fusion.where_ref, s32[384]{0:T(512)S(1)} %reshape.8.offset_ref, s32[8]{0:T(128)S(1)} %get-tuple-element.18.mine_ref, s32[8]{0:T(128)S(1)} %get-tuple-element.19.sent_ref, s32[32]{0:T(128)S(1)} %get-tuple-element.14.index_ref, ...), custom_call_target="tpu_custom_call" | custom-call | tf_op jit(solution)/shard_map/group_pairs/pallas_call | solution.py:666
  68.7 1.2 %copy-done = f32[4,14,40,128]{3,2,1,0:T(8,128)S(1)} copy-done((f32[4,14,40,128]{3,2,1,0:T(8,128)S(1)}, f32[4,14,40,128]{3,2,1,0:T(8,128)}, u32[]{:S(2)}) %copy-start) | copy-done | bytes 1146904
  70.0 3.5 %finish.1 = f32[4,40,1600]{2,1,0:T(8,128)} custom-call(f32[4,14,40,128]{3,2,1,0:T(8,128)S(1)} %copy-done, bf16[8,14,40,128]{3,2,1,0:T(8,128)(2,1)} %all-to-all-done.near_ref, bf16[4,14,40,128]{3,2,1,0:T(8,128)(2,1)S(1)} %collective-permute-done.15.far_ref, s32[8]{0:T(128)S(1)} %get-tuple-element.17.row_ref), custom_call_target="tpu_custom_call" | custom-call | tf_op jit(solution)/shard_map/finish/pallas_call | solution.py:120
  (34 shorter events, 0.8 us)
Async XLA Ops:
  0.8 1.0 %copy-start.1 = (bf16[4,40,1600]{2,1,0:T(8,128)(2,1)S(1)}, bf16[4,40,1600]{2,1,0:T(8,128)(2,1)}, u32[]{:S(2)}) copy-start(bf16[4,40,1600]{2,1,0:T(8,128)(2,1)} %box_ref.1) | copy-start | bytes 1536004
  2.4 9.8 %collective-permute-start.6 = (bf16[2,14,40,128]{3,2,1,0:T(8,128)(2,1)S(1)}, bf16[2,14,40,128]{3,2,1,0:T(8,128)(2,1)S(1)}, u32[]{:S(2)}, u32[]{:S(2)}) collective-permute-start(bf16[2,14,40,128]{3,2,1,0:T(8,128)(2,1)S(1)} %get-tuple-element.11.refs_0_), channel_id=1, source_target_pairs={{0,4},{1,5},{2,6},{3,7},{4,0},{5,1},{6,2},{7,3},{8,12},{9,13},{10,... | collective-permute-start | bytes 860168 | tf_op jit(solution)/shard_map/ppermute | solution.py:694
  3.0 9.8 %collective-permute-start.2 = (bf16[2,14,40,128]{3,2,1,0:T(8,128)(2,1)S(1)}, bf16[2,14,40,128]{3,2,1,0:T(8,128)(2,1)S(1)}, u32[]{:S(2)}, u32[]{:S(2)}) collective-permute-start(bf16[2,14,40,128]{3,2,1,0:T(8,128)(2,1)S(1)} %get-tuple-element.11.refs_0_), channel_id=1, source_target_pairs={{0,2},{1,3},{2,0},{3,1},{4,6},{5,7},{6,4},{7,5},{8,10},{9,11},{10,... | collective-permute-start | bytes 860168 | tf_op jit(solution)/shard_map/ppermute | solution.py:694
  3.1 13.3 %collective-permute-start = (bf16[2,14,40,128]{3,2,1,0:T(8,128)(2,1)S(1)}, bf16[2,14,40,128]{3,2,1,0:T(8,128)(2,1)S(1)}, u32[]{:S(2)}, u32[]{:S(2)}) collective-permute-start(bf16[2,14,40,128]{3,2,1,0:T(8,128)(2,1)S(1)} %get-tuple-element.11.refs_0_), channel_id=1, source_target_pairs={{0,1},{1,0},{2,3},{3,2},{4,5},{5,4},{6,7},{7,6},{8,9},{9,8},{10,11... | collective-permute-start | bytes 860168 | tf_op jit(solution)/shard_map/ppermute | solution.py:694
  3.1 14.1 %collective-permute-start.7 = (bf16[2,14,40,128]{3,2,1,0:T(8,128)(2,1)S(1)}, bf16[2,14,40,128]{3,2,1,0:T(8,128)(2,1)S(1)}, u32[]{:S(2)}, u32[]{:S(2)}) collective-permute-start(bf16[2,14,40,128]{3,2,1,0:T(8,128)(2,1)S(1)} %get-tuple-element.12.refs_1_), channel_id=1, source_target_pairs={{0,4},{1,5},{2,6},{3,7},{4,0},{5,1},{6,2},{7,3},{8,12},{9,13},{10,... | collective-permute-start | bytes 860168 | tf_op jit(solution)/shard_map/ppermute | solution.py:694
  5.0 12.9 %collective-permute-start.3 = (bf16[2,14,40,128]{3,2,1,0:T(8,128)(2,1)S(1)}, bf16[2,14,40,128]{3,2,1,0:T(8,128)(2,1)S(1)}, u32[]{:S(2)}, u32[]{:S(2)}) collective-permute-start(bf16[2,14,40,128]{3,2,1,0:T(8,128)(2,1)S(1)} %get-tuple-element.12.refs_1_), channel_id=1, source_target_pairs={{0,2},{1,3},{2,0},{3,1},{4,6},{5,7},{6,4},{7,5},{8,10},{9,11},{10,... | collective-permute-start | bytes 860168 | tf_op jit(solution)/shard_map/ppermute | solution.py:694
  12.2 17.0 %copy-start.2 = (bf16[2,14,40,128]{3,2,1,0:T(8,128)(2,1)}, bf16[2,14,40,128]{3,2,1,0:T(8,128)(2,1)S(1)}, u32[]{:S(2)}) copy-start(bf16[2,14,40,128]{3,2,1,0:T(8,128)(2,1)S(1)} %collective-permute-done.6.refs_8_) | copy-start | bytes 860164
  12.2 5.9 %collective-permute-start.1 = (bf16[2,14,40,128]{3,2,1,0:T(8,128)(2,1)S(1)}, bf16[2,14,40,128]{3,2,1,0:T(8,128)(2,1)S(1)}, u32[]{:S(2)}, u32[]{:S(2)}) collective-permute-start(bf16[2,14,40,128]{3,2,1,0:T(8,128)(2,1)S(1)} %get-tuple-element.12.refs_1_), channel_id=1, source_target_pairs={{0,1},{1,0},{2,3},{3,2},{4,5},{5,4},{6,7},{7,6},{8,9},{9,8},{10,11... | collective-permute-start | bytes 860168 | tf_op jit(solution)/shard_map/ppermute | solution.py:694
  12.7 16.0 %collective-permute-start.14 = (bf16[4,14,40,128]{3,2,1,0:T(8,128)(2,1)S(1)}, bf16[4,14,40,128]{3,2,1,0:T(8,128)(2,1)}, u32[]{:S(2)}, u32[]{:S(2)}) collective-permute-start(bf16[4,14,40,128]{3,2,1,0:T(8,128)(2,1)S(1)} %get-tuple-element.13), channel_id=1, source_target_pairs={{8,0},{16,8},{24,16},{0,24},{9,1},{17,9},{25,17},{1,25},{10,2},{18... | collective-permute-start | bytes 1720328 | tf_op jit(solution)/shard_map/ppermute | solution.py:682
  16.3 2.3 %collective-permute-start.8 = (bf16[2,14,40,128]{3,2,1,0:T(8,128)(2,1)S(1)}, bf16[2,14,40,128]{3,2,1,0:T(8,128)(2,1)S(1)}, u32[]{:S(2)}, u32[]{:S(2)}) collective-permute-start(bf16[2,14,40,128]{3,2,1,0:T(8,128)(2,1)S(1)} %collective-permute-done.6.refs_8_), channel_id=1, source_target_pairs={{0,1},{1,0},{2,3},{3,2},{4,5},{5,4},{6,7},{7,6},{8,9},{9,8},{10,11... | collective-permute-start | bytes 860168 | tf_op jit(solution)/shard_map/ppermute | solution.py:694
  17.2 12.0 %copy-start.3 = (bf16[2,14,40,128]{3,2,1,0:T(8,128)(2,1)}, bf16[2,14,40,128]{3,2,1,0:T(8,128)(2,1)S(1)}, u32[]{:S(2)}) copy-start(bf16[2,14,40,128]{3,2,1,0:T(8,128)(2,1)S(1)} %collective-permute-done.7.refs_9_) | copy-start | bytes 860164
  17.2 8.5 %collective-permute-start.10 = (bf16[2,14,40,128]{3,2,1,0:T(8,128)(2,1)S(1)}, bf16[2,14,40,128]{3,2,1,0:T(8,128)(2,1)}, u32[]{:S(2)}, u32[]{:S(2)}) collective-permute-start(bf16[2,14,40,128]{3,2,1,0:T(8,128)(2,1)S(1)} %collective-permute-done.2.refs_4_), channel_id=1, source_target_pairs={{0,4},{1,5},{2,6},{3,7},{4,0},{5,1},{6,2},{7,3},{8,12},{9,13},{10,... | collective-permute-start | bytes 860168 | tf_op jit(solution)/shard_map/ppermute | solution.py:694
  18.0 7.8 %collective-permute-start.4 = (bf16[2,14,40,128]{3,2,1,0:T(8,128)(2,1)S(1)}, bf16[2,14,40,128]{3,2,1,0:T(8,128)(2,1)S(1)}, u32[]{:S(2)}, u32[]{:S(2)}) collective-permute-start(bf16[2,14,40,128]{3,2,1,0:T(8,128)(2,1)S(1)} %collective-permute-done.2.refs_4_), channel_id=1, source_target_pairs={{0,1},{1,0},{2,3},{3,2},{4,5},{5,4},{6,7},{7,6},{8,9},{9,8},{10,11... | collective-permute-start | bytes 860168 | tf_op jit(solution)/shard_map/ppermute | solution.py:694
  18.1 9.2 %collective-permute-start.11 = (bf16[2,14,40,128]{3,2,1,0:T(8,128)(2,1)S(1)}, bf16[2,14,40,128]{3,2,1,0:T(8,128)(2,1)}, u32[]{:S(2)}, u32[]{:S(2)}) collective-permute-start(bf16[2,14,40,128]{3,2,1,0:T(8,128)(2,1)S(1)} %collective-permute-done.7.refs_9_), channel_id=1, source_target_pairs={{0,2},{1,3},{2,0},{3,1},{4,6},{5,7},{6,4},{7,5},{8,10},{9,11},{10,... | collective-permute-start | bytes 860168 | tf_op jit(solution)/shard_map/ppermute | solution.py:694
  18.7 10.6 %copy-start.4 = (bf16[2,14,40,128]{3,2,1,0:T(8,128)(2,1)}, bf16[2,14,40,128]{3,2,1,0:T(8,128)(2,1)S(1)}, u32[]{:S(2)}) copy-start(bf16[2,14,40,128]{3,2,1,0:T(8,128)(2,1)S(1)} %collective-permute-done.8.refs_10_) | copy-start | bytes 860164
  18.7 9.7 %collective-permute-start.9 = (bf16[2,14,40,128]{3,2,1,0:T(8,128)(2,1)S(1)}, bf16[2,14,40,128]{3,2,1,0:T(8,128)(2,1)}, u32[]{:S(2)}, u32[]{:S(2)}) collective-permute-start(bf16[2,14,40,128]{3,2,1,0:T(8,128)(2,1)S(1)} %collective-permute-done.7.refs_9_), channel_id=1, source_target_pairs={{0,1},{1,0},{2,3},{3,2},{4,5},{5,4},{6,7},{7,6},{8,9},{9,8},{10,11... | collective-permute-start | bytes 860168 | tf_op jit(solution)/shard_map/ppermute | solution.py:694
  25.7 2.7 %collective-permute-start.5 = (bf16[2,14,40,128]{3,2,1,0:T(8,128)(2,1)S(1)}, bf16[2,14,40,128]{3,2,1,0:T(8,128)(2,1)}, u32[]{:S(2)}, u32[]{:S(2)}) collective-permute-start(bf16[2,14,40,128]{3,2,1,0:T(8,128)(2,1)S(1)} %collective-permute-done.3.refs_5_), channel_id=1, source_target_pairs={{0,1},{1,0},{2,3},{3,2},{4,5},{5,4},{6,7},{7,6},{8,9},{9,8},{10,11... | collective-permute-start | bytes 860168 | tf_op jit(solution)/shard_map/ppermute | solution.py:694
  25.7 3.0 %collective-permute-start.12 = (bf16[2,14,40,128]{3,2,1,0:T(8,128)(2,1)}, bf16[2,14,40,128]{3,2,1,0:T(8,128)(2,1)}, u32[]{:S(2)}, u32[]{:S(2)}) collective-permute-start(bf16[2,14,40,128]{3,2,1,0:T(8,128)(2,1)} %collective-permute-done.10.refs_12_), channel_id=1, source_target_pairs={{0,1},{1,0},{2,3},{3,2},{4,5},{5,4},{6,7},{7,6},{8,9},{9,8},{10,11... | collective-permute-start | bytes 860168 | tf_op jit(solution)/shard_map/ppermute | solution.py:694
  27.3 1.9 %collective-permute-start.13 = (bf16[2,14,40,128]{3,2,1,0:T(8,128)(2,1)}, bf16[2,14,40,128]{3,2,1,0:T(8,128)(2,1)}, u32[]{:S(2)}, u32[]{:S(2)}) collective-permute-start(bf16[2,14,40,128]{3,2,1,0:T(8,128)(2,1)} %collective-permute-done.11.refs_13_), channel_id=1, source_target_pairs={{0,1},{1,0},{2,3},{3,2},{4,5},{5,4},{6,7},{7,6},{8,9},{9,8},{10,11... | collective-permute-start | bytes 860168 | tf_op jit(solution)/shard_map/ppermute | solution.py:694
  37.2 9.9 %copy-start.5 = (s32[1,2,8]{2,1,0:T(2,128)S(1)}, s32[1,2,8]{2,1,0:T(2,128)}, u32[]{:S(2)}) copy-start(s32[1,2,8]{2,1,0:T(2,128)} %param.7) | copy-start | bytes 196
  37.2 9.9 %copy-start.6 = (s32[1,2,8]{2,1,0:T(2,128)S(1)}, s32[1,2,8]{2,1,0:T(2,128)}, u32[]{:S(2)}) copy-start(s32[1,2,8]{2,1,0:T(2,128)} %param.6) | copy-start | bytes 196
  37.2 31.5 %all-to-all-start = ((bf16[8,14,40,128]{3,2,1,0:T(8,128)(2,1)}), bf16[8,14,40,128]{3,2,1,0:T(8,128)(2,1)}, u32[]{:S(2)}, u32[]{:S(2)}) async-start(bf16[8,14,40,128]{3,2,1,0:T(8,128)(2,1)} %get-tuple-element.15), calls=%async_computation | async-start | bytes 2293760 | tf_op jit(solution)/shard_map/all_to_all | solution.py:719
  46.1 22.6 %collective-permute-start.15 = (bf16[4,14,40,128]{3,2,1,0:T(8,128)(2,1)}, bf16[4,14,40,128]{3,2,1,0:T(8,128)(2,1)S(1)}, u32[]{:S(2)}, u32[]{:S(2)}) collective-permute-start(bf16[4,14,40,128]{3,2,1,0:T(8,128)(2,1)} %get-tuple-element.16), channel_id=1, source_target_pairs={{24,0},{0,8},{8,16},{16,24},{25,1},{1,9},{9,17},{17,25},{26,2},{2,... | collective-permute-start | bytes 1720328 | tf_op jit(solution)/shard_map/ppermute | solution.py:682
  68.7 1.3 %copy-start = (f32[4,14,40,128]{3,2,1,0:T(8,128)S(1)}, f32[4,14,40,128]{3,2,1,0:T(8,128)}, u32[]{:S(2)}) copy-start(f32[4,14,40,128]{3,2,1,0:T(8,128)} %group_pairs.1.field_ref) | copy-start | bytes 3440644
